TPU v7x, 128 devices: a whole 4x4x4 slice. The times are simulated.
128 devices in a mesh: tile: 32 (over x, z, core), spare: 4 (over y).
Axes of the slice: x: 4, y: 4, z: 4, core: 2. Of those that a mesh axis runs over, the one named last changes fastest.
Arguments:
- observed: bfloat16 [128, 32, 128, 128], P('tile', 'spare'), may hold values from -6 to 6
- frame_pick: int32 [128, 32], P('tile', 'spare'), may hold values from 0 to 127, as said below
- frame_count: int32 [128], P('tile'), may hold values from 5 to 32, as said below
- incoming: int32 [128], P('tile'), may hold values from 0 to 127, as said below
- start_coefficients: float32 [128, 36], replicated, may hold values from -1.5 to 1.5
- mode_basis: float32 [36, 128, 128], replicated, may hold values from -6 to 6
Outputs:
- restored: float32 [128, 128, 128], P('tile')
- coefficients: float32 [128, 36], replicated
Inputs may be any that keep to these rules, and one draw needn't show every extreme that they name: `frame_pick`: the slots of one patch name distinct frames. `frame_count`: patch 0 uses all 32 slots. `incoming`: A permutation of the patches. Position q (tile index q // 4) takes a patch of the same tile index or of a neighbouring one, with tile indices wrapping around; at most one patch crosses each boundary between neighbouring tile indices in each direction, and when one crosses, one crosses back; the boundary after tile index 0 is crossed in every draw.
All inputs are finite; a program needn't handle non-finite values.
Results may differ from a plain program's by a relative error of at most 0.0003.
Values may be sent and summed in bfloat16 or wider, within the bound.
A program may use at most 128 MiB of HBM per device.

v0:
```python
import math

import jax
import jax.numpy as jnp
from jax import lax
from jax.sharding import PartitionSpec as P

ITERS = 2


GAMMA = 0.5
STEP = 0.25
EPS = 1e-06
FINE = lax.Precision.HIGHEST


def from_behind(x, axis, by):
    size = lax.axis_size(axis)
    return lax.ppermute(x, axis, [(i, (i + by) % size) for i in range(size)])


def dft_tables(pixels):
    indices = jnp.arange(pixels, dtype=jnp.int32)
    products = indices[:, None] * indices[None, :] % pixels
    angles = products.astype(jnp.float32) * (2.0 * math.pi / pixels)
    cosine = jnp.cos(angles)
    sine = jnp.sin(angles)
    forward_left = jnp.stack([jnp.stack([cosine, sine]), jnp.stack([-sine, cosine])])
    forward_right = jnp.stack([jnp.stack([cosine, -sine]), jnp.stack([sine, cosine])])
    real_left = jnp.stack([cosine, -sine])
    inverse_left = jnp.stack([jnp.stack([cosine, -sine]), jnp.stack([sine, cosine])])
    inverse_right = jnp.stack([jnp.stack([cosine, sine]), jnp.stack([-sine, cosine])])
    return (forward_left, forward_right, real_left, inverse_left, inverse_right)


def pupil_mask(pixels):
    offsets = jnp.arange(pixels, dtype=jnp.int32) - pixels // 2
    radial = offsets[:, None] ** 2 + offsets[None, :] ** 2
    return (radial <= (pixels // 4) ** 2).astype(jnp.float32)


def complex_transform(fields, left_op, right_op, factor):
    halfway = jnp.einsum("jkuv,nkvy->njuy", left_op, fields, precision=FINE)
    return jnp.einsum("nkxy,kjyz->njxz", halfway, right_op, precision=FINE) * factor


def real_transform(images, real_left, right_op, factor):
    halfway = jnp.einsum("juv,nvy->njuy", real_left, images, precision=FINE)
    return jnp.einsum("nkxy,kjyz->njxz", halfway, right_op, precision=FINE) * factor


def frame_terms(coef_rows, basis_flat, spectra, tables, aperture):
    pixels = aperture.shape[0]
    phases = jnp.dot(coef_rows, basis_flat, precision=FINE).reshape(-1, pixels, pixels)
    fields = jnp.stack([aperture * jnp.cos(phases), aperture * jnp.sin(phases)], axis=1)
    amplitude = complex_transform(fields, tables[0], tables[1], 1.0 / pixels)
    spread = (amplitude[:, 0] ** 2 + amplitude[:, 1] ** 2) / jnp.sum(aperture)
    transfer = real_transform(spread, tables[2], tables[1], 1.0)
    crossed = jnp.stack(
        [
            spectra[:, 0] * transfer[:, 0] + spectra[:, 1] * transfer[:, 1],
            spectra[:, 1] * transfer[:, 0] - spectra[:, 0] * transfer[:, 1],
        ],
        axis=1,
    )
    powers = transfer[:, 0] ** 2 + transfer[:, 1] ** 2
    return (crossed, powers)


def patch_loss(numer, denom):
    return -jnp.sum((numer[..., 0, :, :] ** 2 + numer[..., 1, :, :] ** 2) / (GAMMA + denom))


def object_image(numer, denom, tables):
    pixels = numer.shape[-1]
    ratio = numer / (GAMMA + denom)[:, None, :, :]
    return complex_transform(ratio, tables[3], tables[4], 1.0 / pixels)[:, 0]


def relocate(own, arrived_left, arrived_right, distance, source_slot):

    def choose(mine, lefts, rights):
        near = distance.reshape((-1,) + (1,) * (mine.ndim - 1))
        picked_own = jnp.take(mine, source_slot, axis=0)
        picked_left = jnp.take(lefts, source_slot, axis=0)
        picked_right = jnp.take(rights, source_slot, axis=0)
        return jnp.where(near == 0, picked_own, jnp.where(near == 1, picked_right, picked_left))

    return jax.tree.map(choose, own, arrived_left, arrived_right)


def combine_frames(numer, denom):
    return lax.psum((numer, denom), "spare")


def update_modes(coef, local_grad):
    gradient = lax.psum(local_grad, ("tile", "spare"))
    spread = jnp.sqrt(jnp.mean(gradient * gradient) + EPS)
    return coef - STEP * gradient / spread


def per_device(observed, frame_pick, frame_count, incoming, start_coefficients, mode_basis):
    pixels = observed.shape[-1]
    tables = dft_tables(pixels)
    aperture = pupil_mask(pixels)
    basis_flat = mode_basis.reshape(mode_basis.shape[0], pixels * pixels)
    frames = start_coefficients.shape[0]
    tile_count = lax.axis_size("tile")
    tile_index = lax.axis_index("tile")
    spare_count = lax.axis_size("spare")
    spare_index = lax.axis_index("spare")
    patch_dev, slot_dev = frame_pick.shape
    source_slot = incoming % patch_dev
    distance = (incoming // patch_dev - tile_index) % tile_count
    own_items = (observed, frame_pick, frame_count)
    came_left = from_behind((observed, frame_pick, frame_count), "tile", 1)
    came_right = from_behind((observed, frame_pick, frame_count), "tile", -1)
    observed, frame_pick, frame_count = relocate(
        own_items, came_left, came_right, distance, source_slot
    )
    local_patches, columns = (patch_dev, slot_dev)
    order = jnp.arange(columns, dtype=jnp.int32)
    weights = (order[None, :] * spare_count + spare_index < frame_count[:, None]).astype(
        jnp.float32
    )
    spectra = real_transform(
        observed.reshape(-1, pixels, pixels).astype(jnp.float32), tables[2], tables[1], 1.0 / pixels
    )
    spectra = spectra.reshape(local_patches, columns, 2, pixels, pixels)
    select = (frame_pick[..., None] == jnp.arange(frames, dtype=jnp.int32)).astype(jnp.float32)

    def full_sums(coef):
        coef_rows = jnp.einsum("pkf,fm->pkm", select, coef, precision=FINE).reshape(
            -1, coef.shape[1]
        )
        crossed, powers = frame_terms(
            coef_rows, basis_flat, spectra.reshape(-1, 2, pixels, pixels), tables, aperture
        )
        crossed = crossed.reshape(local_patches, columns, 2, pixels, pixels)
        powers = powers.reshape(local_patches, columns, pixels, pixels)
        numer = jnp.einsum("pk,pkjxy->pjxy", weights, crossed, precision=FINE)
        denom = jnp.einsum("pk,pkxy->pxy", weights, powers, precision=FINE)
        return (numer, denom)

    coef = start_coefficients
    for iteration in range(ITERS):
        (numer, denom), pull_frames = jax.vjp(full_sums, coef)
        numer, denom = combine_frames(numer, denom)
        loss_pull = jax.vjp(patch_loss, numer, denom)[1]
        cot_numer, cot_denom = loss_pull(jnp.ones((), numer.dtype))
        local_grad = pull_frames((cot_numer, cot_denom))[0]
        coef = update_modes(coef, local_grad)
    numer, denom = full_sums(coef)
    numer, denom = combine_frames(numer, denom)
    objects = object_image(numer, denom, tables)
    return (objects, coef)


def solution(mesh):
    placed = (P("tile", "spare", None, None), P("tile", "spare"), P("tile"), P("tile"), P(), P())
    return jax.shard_map(
        per_device,
        mesh=mesh,
        in_specs=placed,
        out_specs=(P("tile", None, None), P()),
        check_vma=False,
    )
```

profile of v0, /device:TPU:1, one launch (start us, length us, event | category | flops | bytes accessed | tf_op | source)
XLA Modules:
  0.0 557.8 jit_solution(1528912160777400289)
XLA Ops:
  7.2 3.1 collective-permute-start.1
  10.3 1.7 collective-permute-start.5
  12.1 2.5 collective-permute-start.4
  19.1 2.9 gather_fusion.3
  22.1 1.9 slice_bitcast_fusion
  24.1 5.1 collective-permute-start.2
  32.0 16.9 %fusion.177 = (f32[32,128,128]{2,0,1:T(8,128)S(1)}, f32[32,128,128]{2,0,1:T(8,128)S(1)}) fusion(f32[32,36,1]{1,0,2:T(8,128)S(1)} %convolution_bitcast_fusion.6, f32[128,128,36]{1,0,2:T(8,128)S(1)} %slice_bitcast_fusion), kind=kOutput, calls=%fused_computation.278 | convolution fusion | flops 226492416 | bytes 6558208 | tf_op jit(solution)/shard_map/jvp()/dot_general | solution.py:54
  51.3 6.4 %fusion.40 = f32[32,128,2,128,1]{1,3,4,2,0:T(8,128)S(1)} fusion(f32[32,2,128,128,1]{3,0,2,1,4:T(8,128)S(1)} %maximum_bitcast_fusion, f32[1,2,128,128]{2,3,1,0:T(8,128)S(1)} %get-tuple-element.57, f32[1,2,128,128]{2,3,1,0:T(8,128)S(1)} %get-tuple-element.62), kind=kOutput, calls=%fused_computation.59 | convolution fusion | flops 3221291008 | bytes 8650752 | tf_op jit(solution)/shard_map/jvp(jkuv,nkvy->njuy)/dot_general | solution.py:43
  57.7 4.1 fusion.26
  61.9 4.8 fusion.90
  66.7 5.6 %fusion.52 = f32[32,2,128,128]{2,3,0,1:T(8,128)} fusion(f32[32,128,2,128]{1,3,2,0:T(8,128)S(1)} %fusion.90, f32[1,2,128,128]{2,3,0,1:T(8,128)S(1)} %get-tuple-element.63, f32[1,2,128,128]{2,3,0,1:T(8,128)S(1)} %get-tuple-element.56), kind=kOutput, calls=%fused_computation.72 | convolution fusion | flops 3221291008 | bytes 8650752 | tf_op jit(solution)/shard_map/jvp(nkxy,kjyz->njxz)/dot_general | solution.py:49
  72.3 2.9 gather_fusion.5
  75.2 2.9 gather_fusion.4
  78.0 2.1 fusion.114
  80.2 1.8 fusion.147
  82.1 3.8 fusion.27
  85.9 1.6 multiply_add_fusion.4
  89.5 1.3 fusion.4
  90.9 3.7 reshape.403
  94.5 40.0 %all-reduce.31.cloned.1.call-done = (f32[4,2,128,128]{2,3,0,1:T(8,128)}, f32[4,128,128]{1,2,0:T(8,128)}) async-done(((f32[4,2,128,128]{2,3,0,1:T(8,128)}, f32[4,128,128]{1,2,0:T(8,128)}), (f32[4,2,128,128]{2,3,0,1:T(8,128)}, f32[4,128,128]{1,2,0:T(8,128)})) %all-reduce.31.cloned.1.call-update) | async-done | bytes 786448 | tf_op jit(solution)/shard_map/psum | solution.py:93
  136.0 2.9 bitcast_multiply_fusion.11
  139.5 1.7 copy-done.1
  141.2 2.9 negate_multiply_fusion.1
  144.1 6.3 %fusion.38 = f32[32,128,2,128,1]{1,3,4,2,0:T(8,128)S(1)} fusion(f32[32,1,128,128]{2,3,0,1:T(8,128)S(1)} %get-tuple-element.29, f32[32,1,128,128]{2,3,0,1:T(8,128)} %get-tuple-element.30, f32[32,1,128,128]{2,3,0,1:T(8,128)S(1)} %get-tuple-element.28, f32[32,1,128,128]{2,3,0,1:T(8,128)S(1)} %get-tuple-element.27, ...), kind=kOutput, calls=%fused_computation.57 | convolution fusion | flops 3226533888 | bytes 17039360 | tf_op jit(solution)/shard_map/transpose(jvp(nkxy,kjyz->njxz))/dot_general | solution.py:49
  150.4 4.2 fusion.95
  154.7 4.6 fusion.36
  159.3 5.1 fusion.65
  164.4 5.5 copy.22
  169.9 4.6 fusion.85
  174.5 2.6 copy.23
  177.1 2.8 dot_general.174
  179.9 4.5 fusion.188
  184.7 66.6 %psum.58 = f32[128,36]{0,1:T(8,128)S(1)} all-reduce(f32[128,36]{0,1:T(8,128)S(1)} %convolution_bitcast_fusion.3), channel_id=1, replica_groups=mesh['tile'=32,'spare'=4] {'tile','spare'}, use_global_device_ids=true, to_apply=%region_3.7 | all-reduce | flops 4608 | bytes 36864 | tf_op jit(solution)/shard_map/psum | solution.py:97
  252.7 17.1 %fusion.176 = (f32[32,128,128]{2,0,1:T(8,128)S(1)}, f32[32,128,128]{2,0,1:T(8,128)S(1)}) fusion(f32[32,36,1]{1,0,2:T(8,128)S(1)} %convolution_bitcast_fusion.5, f32[128,128,36]{1,0,2:T(8,128)S(1)} %slice_bitcast_fusion), kind=kOutput, calls=%fused_computation.277 | convolution fusion | flops 226492416 | bytes 6558208 | tf_op jit(solution)/shard_map/jvp()/dot_general | solution.py:54
  272.3 6.4 %fusion.34 = f32[32,128,2,128,1]{1,3,4,2,0:T(8,128)S(1)} fusion(f32[32,2,128,128,1]{3,0,2,1,4:T(8,128)S(1)} %maximum_bitcast_fusion.1, f32[1,2,128,128]{2,3,1,0:T(8,128)S(1)} %get-tuple-element.57, f32[1,2,128,128]{2,3,1,0:T(8,128)S(1)} %get-tuple-element.62), kind=kOutput, calls=%fused_computation.53 | convolution fusion | flops 3221291008 | bytes 8650752 | tf_op jit(solution)/shard_map/jvp(jkuv,nkvy->njuy)/dot_general | solution.py:43
  278.7 4.1 fusion.25
  282.8 4.6 fusion.88
  287.4 3.8 fusion.57
  291.3 1.6 multiply_add_fusion.2
  296.4 39.7 %all-reduce.29.cloned.1.call-done = (f32[4,2,128,128]{2,3,0,1:T(8,128)}, f32[4,128,128]{1,2,0:T(8,128)}) async-done(((f32[4,2,128,128]{2,3,0,1:T(8,128)}, f32[4,128,128]{1,2,0:T(8,128)}), (f32[4,2,128,128]{2,3,0,1:T(8,128)}, f32[4,128,128]{1,2,0:T(8,128)})) %all-reduce.29.cloned.1.call-update) | async-done | bytes 786448 | tf_op jit(solution)/shard_map/psum | solution.py:93
  337.6 2.9 bitcast_multiply_fusion.7
  341.1 1.7 copy-done.3
  342.8 2.9 negate_multiply_fusion
  345.7 6.3 %fusion.32 = f32[32,128,2,128,1]{1,3,4,2,0:T(8,128)S(1)} fusion(f32[32,1,128,128]{2,3,0,1:T(8,128)S(1)} %get-tuple-element.23, f32[32,1,128,128]{2,3,0,1:T(8,128)} %get-tuple-element.24, f32[32,1,128,128]{2,3,0,1:T(8,128)S(1)} %get-tuple-element.22, f32[32,1,128,128]{2,3,0,1:T(8,128)S(1)} %get-tuple-element.21, ...), kind=kOutput, calls=%fused_computation.51 | convolution fusion | flops 3226533888 | bytes 17039360 | tf_op jit(solution)/shard_map/transpose(jvp(nkxy,kjyz->njxz))/dot_general | solution.py:49
  352.0 4.2 fusion.93
  356.2 4.8 fusion.30
  361.0 5.1 fusion.68
  366.2 5.5 copy.27
  371.7 4.6 fusion.79
  376.3 2.6 copy.28
  378.9 2.8 dot_general.193
  381.7 4.5 fusion.189
  386.4 66.6 %psum.61 = f32[128,36]{0,1:T(8,128)S(1)} all-reduce(f32[128,36]{0,1:T(8,128)S(1)} %convolution_bitcast_fusion.2), channel_id=1, replica_groups=mesh['tile'=32,'spare'=4] {'tile','spare'}, use_global_device_ids=true, to_apply=%region_7.11 | all-reduce | flops 4608 | bytes 36864 | tf_op jit(solution)/shard_map/psum | solution.py:97
  454.5 17.1 %multiply_bitcast_fusion.3 = (f32[32,1,128,128]{3,0,2,1:T(8,128)S(1)}, f32[32,1,128,128]{3,0,2,1:T(8,128)S(1)}) fusion(f32[128,128]{1,0:T(8,128)S(1)} %fusion.155, f32[32,36,1]{1,0,2:T(8,128)S(1)} %convolution_bitcast_fusion.4, f32[128,128,36]{1,0,2:T(8,128)S(1)} %slice_bitcast_fusion), kind=kOutput, calls=%fused_computation.126 | convolution fusion | flops 227540992 | bytes 6623744 | tf_op jit(solution)/shard_map/dot_general | solution.py:54
  472.1 6.4 %fusion.28 = f32[32,128,2,128,1]{1,3,4,2,0:T(8,128)S(1)} fusion(f32[32,2,128,128,1]{3,0,2,1,4:T(8,128)S(1)} %maximum_bitcast_fusion.2, f32[1,2,128,128]{2,3,1,0:T(8,128)S(1)} %get-tuple-element.57, f32[1,2,128,128]{2,3,1,0:T(8,128)S(1)} %get-tuple-element.62), kind=kOutput, calls=%fused_computation.47 | convolution fusion | flops 3221291008 | bytes 8650752 | tf_op jit(solution)/shard_map/jkuv,nkvy->njuy/dot_general | solution.py:43
  478.5 4.1 fusion.24
  482.6 4.6 fusion.74
  487.3 3.8 fusion.62
  491.1 1.6 multiply_add_fusion.1
  492.7 2.5 pad_maximum_fusion
  495.2 5.5 copy.91
  501.6 5.0 fusion.168
  506.7 40.0 %all-reduce.27.cloned.1.call-done = (f32[4,2,128,128]{3,2,1,0:T(8,128)}, f32[4,128,128]{1,2,0:T(8,128)}) async-done(((f32[4,2,128,128]{3,2,1,0:T(8,128)}, f32[4,128,128]{1,2,0:T(8,128)}), (f32[4,2,128,128]{3,2,1,0:T(8,128)}, f32[4,128,128]{1,2,0:T(8,128)})) %all-reduce.27.cloned.1.call-update) | async-done | bytes 786448 | tf_op jit(solution)/shard_map/psum | solution.py:93
  547.8 1.7 convolution_bitcast_fusion
  (97 shorter events, 27.8 us)
Async XLA Ops:
  7.2 127.4 %all-reduce.31.cloned.1.call-start = ((), (), s32[]{:S(2)}) async-start(), calls=%async_computation.2 | async-start | bytes 1572864 | tf_op jit(solution)/shard_map/psum | solution.py:93
  7.2 16.9 %collective-permute-start.1 = (s32[4]{0:T(128)}, s32[4]{0:T(128)S(1)}, u32[]{:S(2)}, u32[]{:S(2)}) collective-permute-start(s32[4]{0:T(128)} %param.14), channel_id=1, source_target_pairs={{0,4},{4,8},{8,12},{12,16},{16,20},{20,24},{24,28},{28,32},{32,36}... | collective-permute-start | bytes 56 | tf_op jit(solution)/shard_map/ppermute | solution.py:19
  10.3 19.5 %collective-permute-start = (s32[4]{0:T(128)}, s32[4]{0:T(128)S(1)}, u32[]{:S(2)}, u32[]{:S(2)}) collective-permute-start(s32[4]{0:T(128)} %param.14), channel_id=1, source_target_pairs={{0,124},{4,0},{8,4},{12,8},{16,12},{20,16},{24,20},{28,24},{32,28}... | collective-permute-start | bytes 56 | tf_op jit(solution)/shard_map/ppermute | solution.py:19
  10.3 20.3 %collective-permute-start.5 = (s32[4,8]{1,0:T(4,128)}, s32[4,8]{1,0:T(4,128)S(1)}, u32[]{:S(2)}, u32[]{:S(2)}) collective-permute-start(s32[4,8]{1,0:T(4,128)} %param.13), channel_id=1, source_target_pairs={{0,4},{4,8},{8,12},{12,16},{16,20},{20,24},{24,28},{28,32},{32,36}... | collective-permute-start | bytes 392 | tf_op jit(solution)/shard_map/ppermute | solution.py:19
  12.1 19.1 %collective-permute-start.4 = (s32[4,8]{1,0:T(4,128)}, s32[4,8]{1,0:T(4,128)S(1)}, u32[]{:S(2)}, u32[]{:S(2)}) collective-permute-start(s32[4,8]{1,0:T(4,128)} %param.13), channel_id=1, source_target_pairs={{0,124},{4,0},{8,4},{12,8},{16,12},{20,16},{24,20},{28,24},{32,28}... | collective-permute-start | bytes 392 | tf_op jit(solution)/shard_map/ppermute | solution.py:19
  14.5 57.7 %collective-permute-start.3 = (bf16[4,8,128,128]{3,2,1,0:T(8,128)(2,1)}, bf16[4,8,128,128]{3,2,1,0:T(8,128)(2,1)}, u32[]{:S(2)}, u32[]{:S(2)}) collective-permute-start(bf16[4,8,128,128]{3,2,1,0:T(8,128)(2,1)} %param.12), channel_id=1, source_target_pairs={{0,4},{4,8},{8,12},{12,16},{16,20},{20,24},{24,28},{28,32},{32,36}... | collective-permute-start | bytes 3145736 | tf_op jit(solution)/shard_map/ppermute | solution.py:19
  22.1 8.4 %copy-start.17 = (s32[4]{0:T(128)S(1)}, s32[4]{0:T(128)}, u32[]{:S(2)}) copy-start(s32[4]{0:T(128)} %param.15) | copy-start | bytes 52
  22.1 9.7 %copy-start.15 = (f32[128,36]{0,1:T(8,128)S(1)}, f32[128,36]{0,1:T(8,128)}, u32[]{:S(2)}) copy-start(f32[128,36]{0,1:T(8,128)} %param.16) | copy-start | bytes 55300
  24.1 51.1 %collective-permute-start.2 = (bf16[4,8,128,128]{3,2,1,0:T(8,128)(2,1)}, bf16[4,8,128,128]{3,2,1,0:T(8,128)(2,1)}, u32[]{:S(2)}, u32[]{:S(2)}) collective-permute-start(bf16[4,8,128,128]{3,2,1,0:T(8,128)(2,1)} %param.12), channel_id=1, source_target_pairs={{0,124},{4,0},{8,4},{12,8},{16,12},{20,16},{24,20},{28,24},{32,28}... | collective-permute-start | bytes 3145736 | tf_op jit(solution)/shard_map/ppermute | solution.py:19
  48.9 1.3 copy-start.7
  48.9 2.0 copy-start.8
  61.8 4.8 copy-start.11
  82.0 3.8 copy-start.5
  85.9 2.7 copy-start
  90.8 245.3 %all-reduce.29.cloned.1.call-start = ((), (), s32[]{:S(2)}) async-start(), calls=%async_computation.1 | async-start | bytes 1572864 | tf_op jit(solution)/shard_map/psum | solution.py:93
  139.0 2.2 copy-start.1
  144.1 6.3 %copy-start.12 = (f32[32,2,128,128]{2,3,0,1:T(8,128)S(1)}, f32[32,2,128,128]{2,3,0,1:T(8,128)}, u32[]{:S(2)}) copy-start(f32[32,2,128,128]{2,3,0,1:T(8,128)} %copy-done.11) | copy-start | bytes 12582916
  269.9 1.3 copy-start.9
  269.9 2.0 copy-start.10
  282.8 4.6 copy-start.13
  287.4 3.8 copy-start.2
  291.2 2.7 copy-start.6
  296.2 250.5 %all-reduce.27.cloned.1.call-start = ((), (), s32[]{:S(2)}) async-start(), calls=%async_computation | async-start | bytes 1572864 | tf_op jit(solution)/shard_map/psum | solution.py:93
  340.6 2.2 copy-start.3
  345.7 6.3 %copy-start.14 = (f32[32,2,128,128]{2,3,0,1:T(8,128)S(1)}, f32[32,2,128,128]{2,3,0,1:T(8,128)}, u32[]{:S(2)}) copy-start(f32[32,2,128,128]{2,3,0,1:T(8,128)} %copy-done.13) | copy-start | bytes 12582916
  454.3 17.3 %copy-start.16 = (f32[128,36]{0,1:T(8,128)}, f32[128,36]{0,1:T(8,128)S(1)}, u32[]{:S(2)}) copy-start(f32[128,36]{0,1:T(8,128)S(1)} %divide_subtract_fusion) | copy-start | bytes 55300
  487.3 3.8 copy-start.4
Sparse Core Ops, SparseCore 0:
  91.0 43.5 all-reduce.30
  296.3 39.8 all-reduce.28
  506.8 39.8 all-reduce.26
where the time goes:
time: 563 us; the launch traced here: 558 us
  matrix products  174 us (31%)
  blocking collectives  133 us (24%)
  waiting for transfers between devices  120 us (21%)
  local copies, waits for them, and re-layouts  55.5 us (10%)
  other arithmetic  46.8 us (8%)
  between operations  16.1 us (3%)
  starting transfers between devices  12.8 us (2%)
    psum x2, blocking collectives, update_modes(): gradient = lax.psum(local_grad, ('tile', 'spare'))  133 us
    psum x3, waiting for transfers between devices, combine_frames(): return lax.psum((numer, denom), 'spare')  120 us
    dot_general x5, matrix products, frame_terms(): jnp.dot(coef_rows, basis_flat, precision=FINE).reshape(-1, pixels, pixels)  60.3 us
    dot_general x6, matrix products, complex_transform(): halfway = jnp.einsum('jkuv,nkvy->njuy', left_op, fields, precision=FINE)  31.2 us
    dot_general x6, matrix products, real_transform(): jnp.einsum('nkxy,kjyz->njxz', halfway, right_op, precision=FINE) * factor  29.8 us
    dot_general x6, matrix products, real_transform(): halfway = jnp.einsum('juv,nvy->njuy', real_left, images, precision=FINE)  24.2 us
    dot_general x6, matrix products, complex_transform(): jnp.einsum('nkxy,kjyz->njxz', halfway, right_op, precision=FINE) * factor  22.3 us
    ppermute x6, starting transfers between devices, from_behind(): return lax.ppermute(x, axis, [(i, (i + by) % size) for i in range(size)])  12.5 us
  transfers between devices with their start and end apart: 9, of which 3 were waited for; matrix products, arithmetic and copies ran while one was open for 10% of the time, Pallas kernels for 0%

commit v1 on v0

v1 whole, which is shorter than its diff:
```python
import math

import jax
import jax.numpy as jnp
import ml_dtypes
import numpy as np
from jax import lax
from jax.experimental import pallas as pl
from jax.experimental.pallas import tpu as pltpu
from jax.sharding import PartitionSpec as P

MESH = pl.DeviceIdType.MESH
F32 = jnp.float32
BF16 = jnp.bfloat16
NPIX = 128
ITERS = 2
GAMMA = 0.5
STEP = 0.25
EPS = 1e-06
X0, XN = 32, 72
MROWS = 40
FR = 32
QUADS = 8
TILES = 17


def host_tables():
    index = np.arange(NPIX)
    angle = 2.0 * np.pi * (index[:, None] * index[None, :] % NPIX) / NPIX
    c, s = np.cos(angle), np.sin(angle)
    w1 = np.block([[c, -s], [s, c]]) / NPIX
    ma = np.block([[c, s], [-s, c]])
    rows = X0 + np.arange(XN)
    rows[65] = NPIX // 2
    ma = np.concatenate([ma[:, rows], ma[:, NPIX + rows]], axis=1)
    w1 = np.concatenate([w1[32:96], w1[160:224]], axis=0)
    w1t = np.concatenate([w1[64:].T, -w1[:64].T], axis=1)
    ch, sh = c[:, :64], -s[:, :64].copy()
    sh[:, 0] = c[:, 64]
    zero = np.zeros((NPIX, 64))
    rt = np.block([[ch, zero, sh, zero], [zero, ch, zero, sh]])
    m2 = np.block([[c, s], [-s, c]])

    def parts(table, axis):
        high = table.astype(ml_dtypes.bfloat16)
        low = (table - high.astype(np.float64)).astype(ml_dtypes.bfloat16)
        return np.concatenate([high, high, low], axis=axis)

    out = [parts(one, 0) for one in (w1, rt, rt.T, w1t)] + [parts(one, 1) for one in (m2, m2.T, ma, ma.T)]
    off = index - NPIX // 2
    disc = (off[:, None] ** 2 + off[None, :] ** 2 <= (NPIX // 4) ** 2).astype(np.float32)
    mask = np.zeros((XN, 64), np.float32)
    mask[:65] = disc[X0 : X0 + 65, 32:96]
    mask[65, 0] = disc[64, 96]
    mask = np.concatenate([mask, mask], axis=1)
    weight = np.full((NPIX, NPIX), 4.0, np.float32)
    weight[:, 0] = 2.0
    weight[:, 64] = 2.0
    weight[64, 1] = 2.0
    weight[64, 65] = 2.0
    return out, mask, weight, float(disc.sum())


def split(x):
    high = x.astype(BF16)
    return high, (x - high.astype(F32)).astype(BF16)


def split3(x):
    high = x.astype(BF16).astype(F32)
    rest = x - high
    mid = rest.astype(BF16).astype(F32)
    return high, mid, rest - mid


def mm(a, b):
    return jnp.dot(a, b, preferred_element_type=F32)


def mm_nt(a, b):
    return lax.dot_general(a, b, (((1,), (1,)), ((), ())), preferred_element_type=F32)


def right_mul(x, table):
    high, low = split(x)
    return mm(jnp.concatenate([high, low, high], axis=1), table[...])


def left_mul(table, x):
    high, low = split(x)
    return mm(table[...], jnp.concatenate([high, low, high], axis=0))


COS_POLY = (1.0, -4.93480214, 4.05870915, -1.33521195, 0.23493707, -0.02439593)


def horner(poly, z):
    total = poly[-1]
    for one in poly[-2::-1]:
        total = total * z + one
    return total


def unit_field(half_turns, mask):
    k = jnp.floor(half_turns + 0.5)
    r = half_turns - k
    signed = mask * (1.0 - 2.0 * k + 4.0 * jnp.floor(0.5 * k))
    return signed * horner(COS_POLY, r * r)


def lane_mask(width, first):
    lane = lax.broadcasted_iota(jnp.int32, (8, width), 1)
    return (lane % 64) == first


def rows64(arr, fix):
    return jnp.concatenate([arr[:64], fix(arr[64:72]), arr[72:]], axis=0)


def half_spectra(d_pairs):
    real, imag, lone = [], [], []
    at0 = lane_mask(128, 0)[:1]
    for d in d_pairs:
        di = d[:, 128:]
        total = jnp.sum(di, axis=0, keepdims=True)
        lone.append(pltpu.roll(jnp.broadcast_to(total, (8, 128)), 1, 1))
        real.append(d[:, :128])
        imag.append(jnp.where(at0, 0.0, di))
    return (
        jnp.concatenate([jnp.concatenate(real, axis=1), jnp.concatenate(imag, axis=1)], axis=0),
        jnp.concatenate(lone, axis=1),
    )


def put_lone(t, lone):
    row = lax.broadcasted_iota(jnp.int32, (8, 256), 0)
    here = lane_mask(256, 1) & (row == 0)
    return (
        rows64(t[:128], lambda v: jnp.where(here, lone, v)),
        rows64(t[128:], lambda v: jnp.where(here, 0.0, v)),
    )


def adjoint_images(gr, gi, m2t, rtt):
    row = lax.broadcasted_iota(jnp.int32, (8, 256), 0)
    here = lane_mask(256, 1) & (row == 0)
    lone = jnp.where(here, gr[64:72], 0.0)
    gr = rows64(gr, lambda v: jnp.where(here, 0.0, v))
    gi = rows64(gi, lambda v: jnp.where(here, 0.0, v))
    d = left_mul(m2t, jnp.concatenate([gr, gi], axis=0))
    at0 = lane_mask(128, 0)[:1]
    parts = []
    for i in range(2):
        back = pltpu.roll(lone[:, 128 * i : 128 * i + 128], 127, 1)[:1]
        di = jnp.where(at0, back, d[128:, 128 * i : 128 * i + 128])
        parts.append(jnp.concatenate([d[:128, 128 * i : 128 * i + 128], di], axis=1))
    return right_mul(jnp.concatenate(parts, axis=0), rtt)


def frames_of(g):
    pp, kk = g // 4, g % 4
    return [[(2 * pp + h) * 8 + 2 * kk + i for h in range(2)] for i in range(2)]


def h_frame(h, i, half):
    return (2 * (h // 2) + half) * 8 + 4 * (h % 2) + i


def make_kernel(area):
    inv_area = float(np.float32(1.0 / area))

    def prep_spectra(g, observed, rt, m2, spec):
        pairs = []
        for left, right in frames_of(g):
            image = jnp.concatenate([observed[left], observed[right]], axis=1)
            pairs.append(mm(jnp.concatenate([image, image], axis=1), rt[256:768]) * (1.0 / NPIX))
        side, lone = half_spectra(pairs)
        real, imag = put_lone(left_mul(m2, side), lone)
        spec[g, :128, :] = real
        spec[g, 128:, :] = imag

    def prep_basis(i, basis, basis6, last=False):
        lane = lax.broadcasted_iota(jnp.int32, (MROWS, 128), 1)
        halves = []
        for j in range(2):
            if last:
                rows = pltpu.roll(basis[pl.ds(64 - 32 * j, MROWS, stride=XN), :], 96 - 64 * j, 1)
            else:
                one = pltpu.roll(basis[pl.ds(2 * i + j, MROWS, stride=XN), :], 96, 1)
                other = pltpu.roll(basis[pl.ds(2 * i + j + 32, MROWS, stride=XN), :], 32, 1)
                rows = jnp.where(lane < 64, one, other)
            high, mid, low = split3(rows)
            halves.append(
                jnp.concatenate([high, mid, high, low, mid, high, jnp.zeros((16, NPIX), F32)], axis=0)
            )
        basis6[i] = jnp.concatenate(halves, axis=1).astype(BF16)

    def coef_six(coef, onehot):
        high, mid, low = split3(coef[...] * (1.0 / math.pi))
        stack = jnp.concatenate([high, high, mid, high, mid, low, jnp.zeros((16, NPIX), F32)], axis=0)
        return mm_nt(onehot[...].astype(BF16), stack.astype(BF16)).astype(BF16)

    def phases(six, basis6, phi):
        for i in range(TILES):
            both = mm(six[...], basis6[i])
            phi[pl.ds(2 * i * FR, FR), :] = both[:, :128]
            phi[pl.ds((2 * i + 1) * FR, FR), :] = both[:, 128:]

    def frame_field(f, phi, mask):
        lane = lax.broadcasted_iota(jnp.int32, (8, 128), 1)[:1]
        packed = phi[pl.ds(f, 40, stride=FR), :]
        turned = pltpu.roll(packed, 64, 1)
        phase = jnp.concatenate(
            [jnp.where(lane < 64, packed, turned), jnp.where(lane < 64, turned[:32], packed[:32])], axis=0
        )
        phase = jnp.concatenate([phase[:32], phase[40:], phase[32:40]], axis=0)
        return unit_field(phase - jnp.where(lane < 64, 0.0, 0.5), mask[...])

    def modes(dphi, basis6):
        total = None
        for i in range(TILES):
            a = dphi[pl.ds(2 * i * FR, FR), :]
            b = dphi[pl.ds((2 * i + 1) * FR, FR), :]
            high, low = split(jnp.concatenate([a, b], axis=1))
            part = mm_nt(basis6[i, 0 : 2 * MROWS, :], jnp.concatenate([high, low], axis=0))
            total = part if total is None else total + part
        return total

    def forward(h, it, phi, mask, flip, w1, ma, rt, m2, spec, used, field, amp, trans, sums):
        pp = h // 2
        stack = []
        for i in range(4):
            for half in range(2):
                f = h_frame(h, i, half)
                one = frame_field(f, phi, mask)
                field[f] = one
                stack.append(one)
        b = right_mul(jnp.concatenate(stack, axis=0), w1)
        spreads = []
        for i in range(4):
            parts = []
            for half in range(2):
                one = b[XN * (2 * i + half) : XN * (2 * i + half + 1)]
                parts.append(jnp.concatenate([one[:64], one[64:] * flip[...]], axis=0))
            side = jnp.concatenate(
                [
                    jnp.concatenate([parts[0][:, :128], parts[1][:, :128]], axis=1),
                    jnp.concatenate([parts[0][:, 128:], parts[1][:, 128:]], axis=1),
                ],
                axis=0,
            )
            a = left_mul(ma, side)
            amp[4 * h + i] = a
            spreads.append((a[:128] * a[:128] + a[128:] * a[128:]) * inv_area)
        d = right_mul(jnp.concatenate(spreads, axis=0), rt)
        total = [None] * 3
        for j in range(2):
            g = 2 * h + j
            side, lone = half_spectra([d[256 * j : 256 * j + 128], d[256 * j + 128 : 256 * j + 256]])
            tr, ti = put_lone(left_mul(m2, side), lone)
            trans[g, :128, :] = tr
            trans[g, 128:, :] = ti
            sr, si = spec[g, :128, :], spec[g, 128:, :]
            row = 8 * pp + 4 * (h % 2) + 2 * j
            ua, ub = used[pl.ds(row, 1), :], used[pl.ds(row + 1, 1), :]
            for n, v in enumerate((sr * tr + si * ti, si * tr - sr * ti, tr * tr + ti * ti)):
                one = v[:, :128] * ua + v[:, 128:] * ub
                total[n] = one if j == 0 else total[n] + one
        first = h % 2 == 0
        for n in range(3):
            sums[it, pp, n] = jnp.where(first, 0.0, sums[it, pp, n]) + total[n]

    def backward(h, cot, spec, trans, used, flip, m2t, rtt, mat, w1t, amp, field, dphi):
        pp = h // 2
        images = []
        for j in range(2):
            g = 2 * h + j
            row = 8 * pp + 4 * (h % 2) + 2 * j
            u = jnp.concatenate([used[pl.ds(row, 1), :], used[pl.ds(row + 1, 1), :]], axis=1)
            qr, qi, qq = [jnp.concatenate([cot[pp, n], cot[pp, n]], axis=1) for n in range(3)]
            tr, ti = trans[g, :128, :], trans[g, 128:, :]
            sr, si = spec[g, :128, :], spec[g, 128:, :]
            gr = u * (qq * tr - qr * sr - qi * si)
            gi = u * (qi * sr - qr * si + qq * ti)
            images.append(adjoint_images(gr, gi, m2t, rtt))
        stack = []
        for i in range(4):
            a = amp[4 * h + i]
            one = images[i // 2][128 * (i % 2) : 128 * (i % 2) + 128] * (2.0 * inv_area)
            db = left_mul(mat, jnp.concatenate([a[:128] * one, a[128:] * one], axis=0))
            for half in range(2):
                cols = slice(128 * half, 128 * half + 128)
                one = jnp.concatenate([db[:XN, cols], db[XN:, cols]], axis=1)
                stack += [one[:64], one[64:] * flip[...]]
        d = right_mul(jnp.concatenate(stack, axis=0), w1t)
        lane = lax.broadcasted_iota(jnp.int32, (8, 128), 1)[:1]
        for i in range(4):
            for half in range(2):
                f, place = h_frame(h, i, half), 2 * i + half
                v = field[f] * d[XN * place : XN * place + XN]
                v = v + pltpu.roll(v, 64, 1)
                dphi[pl.ds(f, 40, stride=FR), :] = jnp.concatenate(
                    [jnp.where(lane < 64, v[:32], v[32:64]), jnp.where(lane < 64, v[64:], 0.0)], axis=0
                )

    def kernel(
        observed_h, basis_h, pick, count, coef0, incoming, mask, weight, flip,
        right_h, m2_h, ma_h, mat_h, w1_h, w1t_h,
        out, coef_out,
        observed, basis, onehot, used, coef, own, right, left, ma, mat, w1, w1t,
        spec, basis6, six, phi, dphi, field, amp, trans, sums, slots, ratio, cot, grads, objects, near, send, arrive,
        rs_send, rs_recv, ag_send, ag_recv, gr_send, gr_recv, nb_send, nb_recv, basis_sem, load_sem,
    ):
        rt, rtt = right.at[0], right.at[1]
        m2, m2t = left.at[0], left.at[1]
        t, s = lax.axis_index("tile"), lax.axis_index("spare")
        tx, tz, tc = t // 8, (t // 2) % 4, t % 2
        spare_of = [(s + d) % 4 for d in (1, 2, 3)]
        groups = [
            [(t, v) for v in spare_of] + [(t + 1 - 2 * tc, (s + d) % 4) for d in range(4)],
            [(((tx + d) % 4) * 8 + tz * 2 + tc, s) for d in (1, 2, 3)],
            [(tx * 8 + ((tz + d) % 4) * 2 + tc, s) for d in (1, 2, 3)],
        ]
        places = [tc * 4 + s, tx, tz]
        beside = [((t + 1) % 32, s), ((t + 31) % 32, s)]

        barrier = pltpu.get_barrier_semaphore()
        partners = [who for group in groups for who in group] + beside
        for who in partners:
            pl.semaphore_signal(barrier, inc=1, device_id=who, device_id_type=MESH)

        loads = [
            pltpu.make_async_copy(src, dst, load_sem.at[n])
            for n, (src, dst) in enumerate(
                [(observed_h, observed), (right_h, right), (m2_h, left), (ma_h, ma), (mat_h, mat), (w1_h, w1), (w1t_h, w1t)]
            )
        ]
        windows = [
            pltpu.make_async_copy(
                basis_h.at[m, pl.ds(X0, XN), :], basis.at[pl.ds(m * XN, XN), :], basis_sem.at[m]
            )
            for m in range(36)
        ]
        for one in windows + loads:
            one.start()

        def remote(src, dst, ssem, rsem, who):
            return pltpu.make_async_remote_copy(
                src_ref=src, dst_ref=dst, send_sem=ssem, recv_sem=rsem, device_id=who, device_id_type=MESH
            )

        def near_copy(d):
            return remote(own, near.at[d], nb_send.at[0, d], nb_recv.at[0, d], beside[d])

        def object_copy(d):
            return remote(send.at[d], arrive.at[d], nb_send.at[1, d], nb_recv.at[1, d], beside[d])

        def scatter_copy(it, pp, d):
            rows = pl.ds(pl.multiple_of(spare_of[d] * 32, 32), 32)
            return remote(
                sums.at[it, pp, :, rows, :], slots.at[it, pp, d], rs_send.at[it, pp, d], rs_recv.at[it, pp, d], groups[0][d]
            )

        my_rows = pl.ds(pl.multiple_of(s * 32, 32), 32)

        def gather_copy(it, pp, d):
            here = ratio.at[it, pp, :, my_rows, :]
            return remote(here, here, ag_send.at[it, pp, d], ag_recv.at[it, pp, d], groups[0][d])

        def grad_copy(it, stage, d):
            here = grads.at[it, stage, places[stage]]
            return remote(here, here, gr_send.at[it, stage, d], gr_recv.at[it, stage, d], groups[stage][d])

        def scatter_start(it, pp):
            for d in range(3):
                scatter_copy(it, pp, d).start()

        def scatter_finish(it, pp):
            for d in range(3):
                scatter_copy(it, pp, d).wait()
            total = [
                sums[it, pp, j, my_rows, :] + slots[it, pp, 0, j] + slots[it, pp, 1, j] + slots[it, pp, 2, j]
                for j in range(3)
            ]
            scale = 1.0 / (GAMMA + total[2])
            ratio[it, pp, 0, my_rows, :] = total[0] * scale
            ratio[it, pp, 1, my_rows, :] = total[1] * scale
            for d in range(3):
                gather_copy(it, pp, d).start()

        def gather_finish(it, pp):
            for d in range(3):
                gather_copy(it, pp, d).wait()
            qr, qi = ratio[it, pp, 0], ratio[it, pp, 1]
            cot[pp, 0] = weight[...] * qr
            cot[pp, 1] = weight[...] * qi
            cot[pp, 2] = weight[...] * (qr * qr + qi * qi)

        lane = lax.broadcasted_iota(jnp.int32, (8, 128), 1)
        wanted = jnp.full((8, 128), -1, jnp.int32)
        for j in range(4):
            wanted = jnp.where(lane == j, incoming[j], wanted)
        own[...] = wanted
        for f in range(FR):
            onehot[pl.ds(f, 1), :] = jnp.where(lane[:1] == pick[f // 8, f % 8], 1.0, 0.0)
        for row in range(16):
            pair, k = row // 8, row % 8
            bound = jnp.where(lane[:1] < 64, count[2 * pair], count[2 * pair + 1])
            used[pl.ds(row, 1), :] = jnp.where(4 * k + s < bound, 1.0, 0.0)
        coef[...] = jnp.zeros_like(coef)
        coef[0:36, :] = coef0[...]
        basis[pl.ds(36 * XN, 4 * XN), :] = jnp.zeros((4 * XN, NPIX), F32)
        for one in windows:
            one.wait()
        pl.loop(0, TILES - 1)(lambda i: prep_basis(i, basis, basis6))
        prep_basis(TILES - 1, basis, basis6, last=True)
        phi[pl.ds(2 * TILES * FR, 6 * FR), :] = jnp.zeros((6 * FR, 128), F32)
        for one in loads:
            one.wait()
        pl.loop(0, QUADS, unroll=2)(lambda g: prep_spectra(g, observed, rt, m2, spec))
        pl.semaphore_wait(barrier, len(partners))
        for d in range(2):
            near_copy(d).start()

        @pl.loop(0, ITERS + 1)
        def iteration(it):
            six[...] = coef_six(coef, onehot)
            phases(six, basis6, phi)

            @pl.loop(0, QUADS // 2)
            def forward_quads(h):
                forward(h, it, phi, mask, flip, w1, ma, rt, m2, spec, used, field, amp, trans, sums)

                @pl.when(h == 1)
                def _():
                    scatter_start(it, 0)

                @pl.when(h == 2)
                def _():
                    scatter_finish(it, 0)

                @pl.when(h == 3)
                def _():
                    scatter_start(it, 1)
                    gather_finish(it, 0)

            @pl.when(it < ITERS)
            def _():
                @pl.loop(0, QUADS // 2)
                def backward_quads(h):
                    @pl.when(h == 1)
                    def _():
                        scatter_finish(it, 1)

                    @pl.when(h == 2)
                    def _():
                        gather_finish(it, 1)

                    backward(h, cot, spec, trans, used, flip, m2t, rtt, mat, w1t, amp, field, dphi)

                acc = modes(dphi, basis6)
                slot_grad = acc[:MROWS] + acc[MROWS:]
                twice = jnp.concatenate([onehot[...], onehot[...]], axis=0).astype(BF16)
                total = None
                for part in split3(slot_grad):
                    one = mm(part.astype(BF16), twice)
                    total = one if total is None else total + one
                for stage in range(3):
                    grads[it, stage, places[stage]] = total
                    count = len(groups[stage])
                    for d in range(count):
                        grad_copy(it, stage, d).start()
                    for d in range(count):
                        grad_copy(it, stage, d).wait()
                    total = grads[it, stage, 0]
                    for d in range(count):
                        total = total + grads[it, stage, d + 1]
                mean = jnp.sum(total * total) * (1.0 / (128.0 * 36.0))
                coef[...] = coef[...] - STEP * total / jnp.sqrt(jnp.full(total.shape, mean + EPS, F32))

        scatter_finish(ITERS, 1)
        gather_finish(ITERS, 1)
        gr = jnp.concatenate([cot[0, 0], cot[1, 0]], axis=1) * (0.5 / NPIX)
        gi = jnp.concatenate([cot[0, 1], cot[1, 1]], axis=1) * (0.5 / NPIX)
        images = adjoint_images(gr, gi, m2t, rtt)
        for p in range(4):
            objects[p] = images[128 * (p // 2) : 128 * (p // 2) + 128, 128 * (p % 2) : 128 * (p % 2) + 128]

        for d in range(2):
            near_copy(d).wait()
        for d in range(2):
            wanted = near[1 - d]
            total = None
            for p in range(4):
                match = jnp.where(wanted == 4 * t + p, 1.0, 0.0)
                one = jnp.max(match[:1, :], axis=1, keepdims=True) * objects[p]
                total = one if total is None else total + one
            send[d] = total
            object_copy(d).start()
        for d in range(2):
            object_copy(d).wait()
        for j in range(4):
            source = incoming[j]
            total = jnp.where(source // 4 == (t + 31) % 32, arrive[0], arrive[1])
            for p in range(4):
                total = jnp.where(source == 4 * t + p, objects[p], total)
            out[j] = total
        coef_out[...] = coef[0:36, :]

    return kernel


def per_device(observed, frame_pick, frame_count, incoming, start_coefficients, mode_basis):
    tables, mask, weight, area = host_tables()
    flip = np.ones((8, 256), np.float32)
    flip[1, 1::2] = -1.0
    vmem = pl.BlockSpec(memory_space=pltpu.VMEM)
    smem = pl.BlockSpec(memory_space=pltpu.SMEM)
    hbm = pl.BlockSpec(memory_space=pl.ANY)
    dma = pltpu.SemaphoreType.DMA
    steps = ITERS + 1
    objects, coef = pl.pallas_call(
        make_kernel(area),
        out_shape=(
            jax.ShapeDtypeStruct((4, NPIX, NPIX), F32),
            jax.ShapeDtypeStruct((36, 128), F32),
        ),
        in_specs=[hbm, hbm, smem, smem, vmem, smem, vmem, vmem, vmem] + [hbm] * 6,
        out_specs=(vmem, vmem),
        scratch_shapes=[
            pltpu.VMEM((FR, NPIX, NPIX), BF16),
            pltpu.VMEM((MROWS * XN, NPIX), F32),
            pltpu.VMEM((FR, 128), F32),
            pltpu.VMEM((16, 128), F32),
            pltpu.VMEM((MROWS, 128), F32),
            pltpu.VMEM((8, 128), jnp.int32),
            pltpu.VMEM((2, 768, 256), BF16),
            pltpu.VMEM((2, 256, 768), BF16),
            pltpu.VMEM((256, 6 * XN), BF16),
            pltpu.VMEM((2 * XN, 768), BF16),
            pltpu.VMEM((384, 256), BF16),
            pltpu.VMEM((768, 128), BF16),
            pltpu.VMEM((QUADS, 256, 256), F32),
            pltpu.VMEM((TILES, 256, 256), BF16),
            pltpu.VMEM((FR, 256), BF16),
            pltpu.VMEM((40 * FR, 128), F32),
            pltpu.VMEM((40 * FR, 128), F32),
            pltpu.VMEM((FR, XN, 128), F32),
            pltpu.VMEM((2 * QUADS, 256, 256), F32),
            pltpu.VMEM((QUADS, 256, 256), F32),
            pltpu.VMEM((steps, 2, 3, 128, 128), F32),
            pltpu.VMEM((steps, 2, 3, 3, 32, 128), F32),
            pltpu.VMEM((steps, 2, 2, 128, 128), F32),
            pltpu.VMEM((2, 3, 128, 128), F32),
            pltpu.VMEM((ITERS, 3, 8, MROWS, 128), F32),
            pltpu.VMEM((4, 128, 128), F32),
            pltpu.VMEM((2, 8, 128), jnp.int32),
            pltpu.VMEM((2, 128, 128), F32),
            pltpu.VMEM((2, 128, 128), F32),
            dma((steps, 2, 3)),
            dma((steps, 2, 3)),
            dma((steps, 2, 3)),
            dma((steps, 2, 3)),
            dma((ITERS, 3, 7)),
            dma((ITERS, 3, 7)),
            dma((2, 2)),
            dma((2, 2)),
            dma((36,)),
            dma((7,)),
        ],
        compiler_params=pltpu.CompilerParams(
            collective_id=0, has_side_effects=True, vmem_limit_bytes=56 * 1024 * 1024
        ),
        cost_estimate=pl.CostEstimate(flops=30_000_000_000, bytes_accessed=10_000_000, transcendentals=0),
    )(
        observed.reshape(FR, NPIX, NPIX), mode_basis, frame_pick, frame_count, start_coefficients.T, incoming,
        jnp.asarray(mask), jnp.asarray(weight), jnp.asarray(flip),
        jnp.asarray(np.stack(tables[1:3])), jnp.asarray(np.stack(tables[4:6])),
        *[jnp.asarray(tables[n]) for n in (6, 7, 0, 3)],
    )
    return objects, coef.T


def solution(mesh):
    placed = (P("tile", "spare", None, None), P("tile", "spare"), P("tile"), P("tile"), P(), P())
    return jax.shard_map(
        per_device,
        mesh=mesh,
        in_specs=placed,
        out_specs=(P("tile", None, None), P()),
        check_vma=False,
    )
```

time: 563 us -> 113 us (0.20)
  matrix products: 174 us -> 0 us
  blocking collectives: 133 us -> 0 us
  waiting for transfers between devices: 120 us -> 0 us
  Pallas kernels: 0 us -> 109 us
  local copies, waits for them, and re-layouts: 55.5 us -> 3 us
  other arithmetic: 46.8 us -> 0 us
  between operations: 16.1 us -> 0.64 us
  starting transfers between devices: 12.8 us -> 0 us
    dot_general x35 -> x0, matrix products: 174 us -> none  [the longest x5 60.3 us: frame_terms(): jnp.dot(coef_rows, basis_flat, precision=FINE).reshape(-1, pixels, pixels)]
    psum x2 -> x0, blocking collectives: 133 us -> none  [update_modes(): gradient = lax.psum(local_grad, ('tile', 'spare'))]
    psum x3 -> x0, waiting for transfers between devices: 120 us -> none  [combine_frames(): return lax.psum((numer, denom), 'spare')]
    pallas_call x0 -> x1, Pallas kernels: none -> 109 us  [per_device(): pl.pallas_call(make_kernel(area), out_shape=(jax.ShapeDtypeStruct((4, NPI...]
    dot_general x5 -> x0, local copies, waits for them, and re-layouts: 18.6 us -> none  [the longest x2 11.1 us: complex_transform(): halfway = jnp.einsum('jkuv,nkvy->njuy', left_op, fields, precision=FINE)]
    gather x9 -> x0, local copies, waits for them, and re-layouts: 13.6 us -> none  [the longest x3 5.48 us: choose(): picked_own = jnp.take(mine, source_slot, axis=0)]
    ppermute x6 -> x0, starting transfers between devices: 12.5 us -> none  [from_behind(): return lax.ppermute(x, axis, [(i, (i + by) % size) for i in range(size)])]
    mul x4 -> x0, other arithmetic: 11.6 us -> none  [the longest x2 5.81 us: frame_terms(): powers = transfer[:, 0] ** 2 + transfer[:, 1] ** 2]
  transfers between devices with their start and end apart: 9 -> 0, of which waited for: 3 -> 0; matrix products, arithmetic and copies ran while one was open for 10% -> 0% of each run, Pallas kernels for 0% -> 0%
where the time goes in v1:
time: 113 us
  Pallas kernels  109 us (96%)
  local copies, waits for them, and re-layouts  3 us (3%)
    pallas_call x1, Pallas kernels, per_device(): pl.pallas_call(make_kernel(area), out_shape=(jax.ShapeDtypeStruct((4, NPI...  109 us
    unnamed x2, local copies, waits for them, and re-layouts  3 us

profile of v1, /device:TPU:1, one launch (start us, length us, event | category | flops | bytes accessed | tf_op | source)
XLA Modules:
  0.0 112.9 jit_solution(11358245108620453221)
XLA Ops:
  0.6 109.3 %shard_map.158 = (f32[4,128,128]{2,1,0:T(8,128)}, f32[36,128]{1,0:T(8,128)}) custom-call(bf16[32,128,128]{2,1,0:T(8,128)(2,1)} %bitcast.4, f32[36,128,128]{2,1,0:T(8,128)} %basis_h.1, s32[4,8]{1,0:T(4,128)} %pick.1, s32[4]{0:T(128)} %count.1, f32[36,128]{1,0:T(8,128)} %bitcast.5, s32[4]{0:T(128)} %incoming.1, f32[72,128]{1,0:T(8,128)} %constant.18.clone.mask, ...), custom_call_target="tpu_custom_call" | custom-call | flops 30000001024 | bytes 10000000 | tf_op jit(solution)/shard_map/pallas_call | solution.py:522
  109.9 1.7 %copy.19 = f32[4,128,128]{2,1,0:T(8,128)} copy(f32[4,128,128]{2,1,0:T(8,128)} %get-tuple-element.8) | data formatting | bytes 524288
  111.6 1.3 %copy.20 = f32[128,36]{0,1:T(8,128)} copy(f32[128,36]{0,1:T(8,128)} %bitcast.3) | data formatting | bytes 36864

commit v2 on v1

v2 whole, which is shorter than its diff:
```python
import math

import jax
import jax.numpy as jnp
import ml_dtypes
import numpy as np
from jax import lax
from jax.experimental import pallas as pl
from jax.experimental.pallas import tpu as pltpu
from jax.sharding import PartitionSpec as P

MESH = pl.DeviceIdType.MESH
F32 = jnp.float32
BF16 = jnp.bfloat16
NPIX = 128
ITERS = 2
GAMMA = 0.5
STEP = 0.25
EPS = 1e-06
X0, XN = 32, 72
MROWS = 40
FR = 32
QUADS = 8
PAIRS = 4
STEPS = 16 // PAIRS
TILES = 17


def host_tables():
    index = np.arange(NPIX)
    angle = 2.0 * np.pi * (index[:, None] * index[None, :] % NPIX) / NPIX
    c, s = np.cos(angle), np.sin(angle)
    off = index - NPIX // 2
    disc = (off[:, None] ** 2 + off[None, :] ** 2 <= (NPIX // 4) ** 2).astype(np.float32)
    area = float(disc.sum())

    def two(table):
        high = table.astype(ml_dtypes.bfloat16)
        return high, (table - high.astype(np.float64)).astype(ml_dtypes.bfloat16)

    def wide(table, extra=0):
        high, low = two(table)
        return np.concatenate([high, high, low, np.zeros((len(table), extra), high.dtype)], axis=1)

    def tall(table):
        high, low = two(table)
        return np.concatenate([high, high, low], axis=0)

    def beside(table):
        return np.concatenate(two(table), axis=1)

    w1 = np.block([[c[32:96], -s[32:96]], [s[32:96], c[32:96]]]) / (NPIX * math.sqrt(area))
    w1t = np.concatenate([w1[64:].T, -w1[:64].T], axis=1)
    rows = np.concatenate([c[:64], c[64:65], s[1:64]], axis=0)
    order = np.concatenate([np.arange(65), 128 - np.arange(1, 64)])
    pupil = X0 + np.arange(XN)
    pupil[65] = NPIX // 2
    a2 = rows[:, pupil]
    a2t = np.concatenate([a2.T, np.zeros((8, NPIX))], axis=0)
    t2 = rows[:, order]
    cosine, sine = c[:, :64], -s[:, :64].copy()
    sine[:, 0] = c[:, 64]
    left, right = np.concatenate([cosine, sine], axis=1), np.concatenate([sine, cosine], axis=1)

    def twice(table):
        one = beside(table)
        return np.concatenate([one, one], axis=0)

    tables = [
        np.stack([twice(left), twice(right), twice(2.0 * left.T), twice(2.0 * right.T)]),
        np.stack([wide(t2), wide(t2.T), wide(rows), wide(rows.T)]),
        wide(a2, 8),
        wide(a2t),
        tall(w1),
        beside(w1t),
    ]
    mask = np.zeros((XN, 64), np.float32)
    mask[:65] = disc[X0 : X0 + 65, 32:96]
    mask[65, 0] = disc[64, 96]
    mask = np.concatenate([mask, mask], axis=1)
    weight = np.full((NPIX, NPIX), 4.0, np.float32)
    weight[:, 0] = 2.0
    weight[:, 64] = 2.0
    weight[64, 1] = 2.0
    weight[64, 65] = 2.0
    flip = np.ones((8, 256), np.float32)
    flip[1, 1::2] = -1.0
    return tables, mask, weight, flip


def split(x):
    high = x.astype(BF16)
    return high, (x - high.astype(F32)).astype(BF16)


def split3(x):
    high = x.astype(BF16).astype(F32)
    rest = x - high
    mid = rest.astype(BF16).astype(F32)
    return high, mid, rest - mid


def mm(a, b):
    return jnp.dot(a, b, preferred_element_type=F32)


def mm_nt(a, b):
    return lax.dot_general(a, b, (((1,), (1,)), ((), ())), preferred_element_type=F32)


def right_mul(x, table):
    high, low = split(x)
    return mm(jnp.concatenate([high, low, high], axis=1), table[...])


def left_mul(table, x):
    high, low = split(x)
    return mm(table[...], jnp.concatenate([high, low, high], axis=0))


def left_pupil(table, x):
    high = x.astype(BF16).astype(F32)
    zero = jnp.zeros((8, x.shape[1]), F32)
    return mm(table[...], jnp.concatenate([high, x - high, high, zero], axis=0).astype(BF16))


def lanes_mul(x, table):
    both = mm(jnp.concatenate(split(x), axis=1), table[...])
    return both[:, :128] + both[:, 128:]


def row0(v, first):
    here = lax.broadcasted_iota(jnp.int32, (8, v.shape[1]), 0) == 0
    return jnp.concatenate([jnp.where(here, first, v[:8]), v[8:]], axis=0)


def unfold(real, imag):
    cr, sr, ci, si = real[:64], real[64:], imag[:64], imag[64:]
    sr0, si0 = row0(sr, 0.0), row0(si, 0.0)
    return (
        jnp.concatenate([cr + si0, row0(cr - si0, sr[:8])], axis=0),
        jnp.concatenate([ci - sr0, row0(ci + sr0, si[:8])], axis=0),
    )


def fold(gr, gi):
    ga, gb, ha, hb = gr[:64], gr[64:], gi[:64], gi[64:]
    return (
        jnp.concatenate([row0(ga + gb, ga[:8]), row0(hb - ha, gb[:8])], axis=0),
        jnp.concatenate([row0(ha + hb, ha[:8]), row0(ga - gb, hb[:8])], axis=0),
    )


COS_POLY = (1.0, -4.93480214, 4.05870915, -1.33521195, 0.23493707, -0.02439593)


def horner(poly, z):
    total = poly[-1]
    for one in poly[-2::-1]:
        total = total * z + one
    return total


def unit_field(half_turns, mask):
    k = jnp.floor(half_turns + 0.5)
    r = half_turns - k
    signed = mask * (1.0 - 2.0 * k + 4.0 * jnp.floor(0.5 * k))
    return signed * horner(COS_POLY, r * r)


def lane_mask(width, first):
    lane = lax.broadcasted_iota(jnp.int32, (8, width), 1)
    return (lane % 64) == first


def rows64(arr, fix):
    return jnp.concatenate([arr[:64], fix(arr[64:72]), arr[72:]], axis=0)


def left_half():
    return lax.broadcasted_iota(jnp.int32, (8, 128), 1)[:1] < 64


def half_spectra(lefts, rights, t2):
    low, at0 = left_half(), lane_mask(128, 0)[:1]
    lone, real, imag = [], [], []
    for one, two in zip(lefts, rights):
        di = pltpu.roll(jnp.where(low, two, one), 64, 1)
        total = jnp.sum(di, axis=0, keepdims=True)
        lone.append(pltpu.roll(jnp.broadcast_to(total, (8, 128)), 1, 1))
        real.append(jnp.where(low, one, two))
        imag.append(jnp.where(at0, 0.0, di))
    tr, ti = unfold(left_mul(t2, jnp.concatenate(real, axis=1)), left_mul(t2, jnp.concatenate(imag, axis=1)))
    here = lane_mask(256, 1) & (lax.broadcasted_iota(jnp.int32, (8, 256), 0) == 0)
    lone = jnp.concatenate(lone, axis=1)
    return rows64(tr, lambda v: jnp.where(here, lone, v)), rows64(ti, lambda v: jnp.where(here, 0.0, v))


def adjoint_lanes(gr, gi, t2t):
    width = gr.shape[1]
    here = lane_mask(width, 1) & (lax.broadcasted_iota(jnp.int32, (8, width), 0) == 0)
    lone = jnp.where(here, gr[64:72], 0.0)
    xr, xi = fold(
        rows64(gr, lambda v: jnp.where(here, 0.0, v)), rows64(gi, lambda v: jnp.where(here, 0.0, v))
    )
    dr, di = left_mul(t2t, xr), left_mul(t2t, xi)
    low, at0 = left_half(), lane_mask(128, 0)[:1]
    lefts, rights = [], []
    for i in range(width // 128):
        cols = slice(128 * i, 128 * i + 128)
        back = pltpu.roll(lone[:, cols], 127, 1)[:1]
        turned = pltpu.roll(jnp.where(at0, back, di[:, cols]), 64, 1)
        lefts.append(jnp.where(low, dr[:, cols], turned))
        rights.append(jnp.where(low, turned, dr[:, cols]))
    return lefts, rights


def rows_of(x, n):
    return x[128 * n : 128 * n + 128]


def make_kernel():
    def prep_spectra(source, observed, t1, t2, spec):
        sides = []
        for half in range(2):
            both = [mm(observed[source, 2 * i + half], t1[half, 0:128, :]) for i in range(4)]
            sides.append([(one[:, :128] + one[:, 128:]) * (1.0 / NPIX) for one in both])
        for j in range(2):
            real, imag = half_spectra(sides[0][2 * j : 2 * j + 2], sides[1][2 * j : 2 * j + 2], t2)
            spec[2 * source + j, :128, :] = real
            spec[2 * source + j, 128:, :] = imag

    def prep_basis(i, basis, basis6, last=False):
        lane = lax.broadcasted_iota(jnp.int32, (MROWS, 128), 1)
        halves = []
        for j in range(2):
            if last:
                rows = pltpu.roll(basis[pl.ds(64 - 32 * j, MROWS, stride=XN), :], 96 - 64 * j, 1)
            else:
                one = pltpu.roll(basis[pl.ds(2 * i + j, MROWS, stride=XN), :], 96, 1)
                other = pltpu.roll(basis[pl.ds(2 * i + j + 32, MROWS, stride=XN), :], 32, 1)
                rows = jnp.where(lane < 64, one, other)
            high, mid, low = split3(rows)
            halves.append(
                jnp.concatenate([high, mid, high, low, mid, high, jnp.zeros((16, NPIX), F32)], axis=0)
            )
        basis6[i] = jnp.concatenate(halves, axis=1).astype(BF16)

    def coef_six(coef, onehot):
        high, mid, low = split3(coef[...] * (1.0 / math.pi))
        stack = jnp.concatenate([high, high, mid, high, mid, low, jnp.zeros((16, NPIX), F32)], axis=0)
        return mm_nt(onehot[...].astype(BF16), stack.astype(BF16)).astype(BF16)

    def phases(six, basis6, phi):
        for i in range(TILES):
            both = mm(six[...], basis6[i])
            phi[pl.ds(2 * i * FR, FR), :] = both[:, :128]
            phi[pl.ds((2 * i + 1) * FR, FR), :] = both[:, 128:]

    def frame_field(f, phi, mask):
        lane = lax.broadcasted_iota(jnp.int32, (8, 128), 1)[:1]
        packed = phi[pl.ds(f, 40, stride=FR), :]
        turned = pltpu.roll(packed, 64, 1)
        phase = jnp.concatenate(
            [jnp.where(lane < 64, packed, turned), jnp.where(lane < 64, turned[:32], packed[:32])], axis=0
        )
        phase = jnp.concatenate([phase[:32], phase[40:], phase[32:40]], axis=0)
        return unit_field(phase - jnp.where(lane < 64, 0.0, 0.5), mask[...])

    def modes(dphi, basis6):
        total = None
        for i in range(TILES):
            a = dphi[pl.ds(2 * i * FR, FR), :]
            b = dphi[pl.ds((2 * i + 1) * FR, FR), :]
            high, low = split(jnp.concatenate([a, b], axis=1))
            part = mm_nt(basis6[i, 0 : 2 * MROWS, :], jnp.concatenate([high, low], axis=0))
            total = part if total is None else total + part
        return total

    def forward(h, phi, mask, flip, w1, a2, t1, t2, field, amp, trans):
        stack = []
        for i in range(PAIRS):
            for half in range(2):
                f = 2 * (PAIRS * h + i) + half
                one = frame_field(f, phi, mask)
                field[f] = one
                stack.append(one)
        b = right_mul(jnp.concatenate(stack, axis=0), w1)
        spreads = [[], []]
        for i in range(PAIRS):
            parts = []
            for half in range(2):
                one = b[XN * (2 * i + half) : XN * (2 * i + half + 1)]
                parts.append(jnp.concatenate([one[:64], one[64:] * flip[...]], axis=0))
            ar, ai = unfold(
                left_pupil(a2, jnp.concatenate([parts[0][:, :128], parts[1][:, :128]], axis=1)),
                left_pupil(a2, jnp.concatenate([parts[0][:, 128:], parts[1][:, 128:]], axis=1)),
            )
            amp[PAIRS * h + i, :128, :] = ar
            amp[PAIRS * h + i, 128:, :] = ai
            spread = ar * ar + ai * ai
            for half in range(2):
                spreads[half].append(spread[:, 128 * half : 128 * half + 128])
        d = [lanes_mul(jnp.concatenate(spreads[half], axis=0), t1.at[half]) for half in range(2)]
        for j in range(PAIRS // 2):
            g = PAIRS // 2 * h + j
            tr, ti = half_spectra(*[[rows_of(d[half], 2 * j), rows_of(d[half], 2 * j + 1)] for half in range(2)], t2)
            trans[g, :128, :] = tr
            trans[g, 128:, :] = ti

    def products(r, trans, spec, used, weight, cot):
        nr = ni = de = None
        upper, lower = pl.ds(pl.multiple_of(16 * r, 16), 16), pl.ds(pl.multiple_of(128 + 16 * r, 16), 16)
        for g in range(QUADS):
            u = used[g : g + 1, :]
            tr, ti, sr, si = trans[g, upper, :], trans[g, lower, :], spec[g, upper, :], spec[g, lower, :]
            vr, vi = tr * u, ti * u
            one = (sr * vr + si * vi, si * vr - sr * vi, tr * vr + ti * vi)
            nr, ni, de = one if g == 0 else (nr + one[0], ni + one[1], de + one[2])
        total = []
        for v in (nr, ni, de):
            v = v[:, :128] + v[:, 128:]
            total.append(v + pltpu.roll(v, 64, 1))
        scale = 1.0 / (GAMMA + total[2])
        qr, qi = total[0] * scale, total[1] * scale
        w = weight[upper, :]
        cot[0, upper, :] = w * qr
        cot[1, upper, :] = w * qi
        cot[2, upper, :] = w * (qr * qr + qi * qi)

    def backward(h, cot, spec, trans, used, flip, t2t, t1, a2t, w1t, amp, field, dphi):
        qr, qi, qq = [jnp.concatenate([cot[n], cot[n]], axis=1) for n in range(3)]
        sides = [[], []]
        for j in range(PAIRS // 2):
            g = PAIRS // 2 * h + j
            u = used[pl.ds(g, 1), :]
            tr, ti = trans[g, :128, :], trans[g, 128:, :]
            sr, si = spec[g, :128, :], spec[g, 128:, :]
            gr = u * (qq * tr - qr * sr - qi * si)
            gi = u * (qi * sr - qr * si + qq * ti)
            for half, one in enumerate(adjoint_lanes(gr, gi, t2t)):
                sides[half] += one
        ds = [lanes_mul(jnp.concatenate(sides[half], axis=0), t1.at[2 + half]) for half in range(2)]
        stack = []
        for i in range(PAIRS):
            one = jnp.concatenate([rows_of(ds[0], i), rows_of(ds[1], i)], axis=1)
            xr, xi = fold(amp[PAIRS * h + i, :128, :] * one, amp[PAIRS * h + i, 128:, :] * one)
            dbr, dbi = left_mul(a2t, xr), left_mul(a2t, xi)
            for half in range(2):
                cols = slice(128 * half, 128 * half + 128)
                one = jnp.concatenate([dbr[:XN, cols], dbi[:XN, cols]], axis=1)
                stack += [one[:64], one[64:] * flip[...]]
        x = jnp.concatenate(stack, axis=0)
        n = x.shape[0]
        both = mm(jnp.concatenate(split(x), axis=0), w1t[...])
        d = both[:n, :128] + both[:n, 128:] + both[n:, :128] + both[n:, 128:]
        lane = lax.broadcasted_iota(jnp.int32, (8, 128), 1)[:1]
        for i in range(PAIRS):
            for half in range(2):
                f, place = 2 * (PAIRS * h + i) + half, 2 * i + half
                v = field[f] * d[XN * place : XN * place + XN]
                v = v + pltpu.roll(v, 64, 1)
                dphi[pl.ds(f, 40, stride=FR), :] = jnp.concatenate(
                    [jnp.where(lane < 64, v[:32], v[32:64]), jnp.where(lane < 64, v[64:], 0.0)], axis=0
                )

    def kernel(
        observed_h, basis_h, pick, count, coef0, incoming, mask, weight, flip,
        t1_h, t2_h, a2_h, a2t_h, w1_h, w1t_h,
        out, coef_out,
        observed, basis, picks, picked, onehot, used, coef, own, t1, t2, a2, a2t, w1, w1t,
        spec, basis6, six, phi, dphi, field, amp, trans, cot, grads, objects, near, send, arrive,
        ob_send, ob_recv, pk_send, pk_recv, gr_send, gr_recv, ag_send, ag_recv, nb_send, nb_recv, basis_sem, load_sem,
    ):
        t, s = lax.axis_index("tile"), lax.axis_index("spare")
        tx, tz, tc = t // 8, (t // 2) % 4, t % 2
        spare_of = [(s + d) % 4 for d in (1, 2, 3)]
        groups = [
            [(t, v) for v in spare_of] + [(t + 1 - 2 * tc, (s + d) % 4) for d in range(4)],
            [(((tx + d) % 4) * 8 + tz * 2 + tc, s) for d in (1, 2, 3)],
            [(tx * 8 + ((tz + d) % 4) * 2 + tc, s) for d in (1, 2, 3)],
        ]
        places = [tc * 4 + s, tx, tz]
        beside = [((t + 1) % 32, s), ((t + 31) % 32, s)]

        barrier = pltpu.get_barrier_semaphore()
        partners = [who for group in groups for who in group] + beside
        for who in partners:
            pl.semaphore_signal(barrier, inc=1, device_id=who, device_id_type=MESH)

        loads = [
            pltpu.make_async_copy(src, dst, load_sem.at[n])
            for n, (src, dst) in enumerate(
                [(observed_h.at[s], observed.at[s]), (t1_h, t1), (t2_h, t2), (a2_h, a2), (a2t_h, a2t), (w1_h, w1), (w1t_h, w1t)]
            )
        ]
        windows = [
            pltpu.make_async_copy(
                basis_h.at[m, pl.ds(X0, XN), :], basis.at[pl.ds(m * XN, XN), :], basis_sem.at[m]
            )
            for m in range(36)
        ]
        for one in windows + loads:
            one.start()

        def remote(src, dst, ssem, rsem, who):
            return pltpu.make_async_remote_copy(
                src_ref=src, dst_ref=dst, send_sem=ssem, recv_sem=rsem, device_id=who, device_id_type=MESH
            )

        def near_copy(d):
            return remote(own, near.at[d], nb_send.at[0, d], nb_recv.at[0, d], beside[d])

        def object_copy(d):
            return remote(send.at[d], arrive.at[d], nb_send.at[1, d], nb_recv.at[1, d], beside[d])

        def frames_copy(d):
            return remote(observed_h.at[spare_of[d]], observed.at[s], ob_send.at[d], ob_recv.at[d], groups[0][d])

        def picks_copy(d):
            return remote(picks.at[spare_of[d]], picked.at[s], pk_send.at[d], pk_recv.at[d], groups[0][d])

        def gather_copy(d):
            return remote(objects.at[s], objects.at[s], ag_send.at[d], ag_recv.at[d], groups[0][d])

        def grad_copy(it, stage, d):
            here = grads.at[it, stage, places[stage]]
            return remote(here, here, gr_send.at[it, stage, d], gr_recv.at[it, stage, d], groups[stage][d])

        lane = lax.broadcasted_iota(jnp.int32, (8, 128), 1)
        row = lax.broadcasted_iota(jnp.int32, (8, 128), 0)
        wanted = jnp.full((8, 128), -1, jnp.int32)
        for j in range(4):
            wanted = jnp.where(lane == j, incoming[j], wanted)
        own[...] = wanted
        for p in range(4):
            spread = jnp.full((8, 128), pick[p, 0], jnp.int32)
            for k in range(1, 8):
                spread = jnp.where(row == k, pick[p, k], spread)
            picks[p] = spread
        picked[s] = picks[s]
        pl.semaphore_wait(barrier, len(partners))
        for d in range(3):
            picks_copy(d).start()
        for d in (1, 0, 2):
            frames_copy(d).start()
        for d in range(2):
            near_copy(d).start()

        lane2 = lax.broadcasted_iota(jnp.int32, (8, 256), 1)
        row2 = lax.broadcasted_iota(jnp.int32, (8, 256), 0)
        used[...] = jnp.where(4 * (4 * (row2 % 2) + lane2 // 64) + row2 // 2 < count[s], 1.0, 0.0)
        coef[...] = jnp.zeros_like(coef)
        coef[0:36, :] = coef0[...]
        basis[pl.ds(36 * XN, 4 * XN), :] = jnp.zeros((4 * XN, NPIX), F32)
        phi[pl.ds(2 * TILES * FR, 6 * FR), :] = jnp.zeros((6 * FR, 128), F32)
        for one in windows:
            one.wait()
        pl.loop(0, TILES - 1)(lambda i: prep_basis(i, basis, basis6))
        prep_basis(TILES - 1, basis, basis6, last=True)
        for d in range(3):
            picks_copy(d).wait()
        for a in range(4):
            onehot[8 * a : 8 * a + 8, :] = jnp.where(picked[a] == lane, 1.0, 0.0)
        for one in loads:
            one.wait()

        @pl.loop(0, ITERS + 1)
        def iteration(it):
            six[...] = coef_six(coef, onehot)
            phases(six, basis6, phi)

            pl.loop(0, STEPS)(lambda h: forward(h, phi, mask, flip, w1, a2, t1, t2.at[0], field, amp, trans))

            @pl.when(it == 0)
            def _():
                prep_spectra(s, observed, t1, t2.at[2], spec)
                for d in (0, 2, 1):
                    frames_copy(d).wait()
                    prep_spectra((s + 3 - d) % 4, observed, t1, t2.at[2], spec)

            pl.loop(0, 8)(lambda r: products(r, trans, spec, used, weight, cot))

            @pl.when(it < ITERS)
            def _():
                pl.loop(0, STEPS)(
                    lambda h: backward(h, cot, spec, trans, used, flip, t2.at[1], t1, a2t, w1t, amp, field, dphi)
                )
                acc = modes(dphi, basis6)
                slot_grad = acc[:MROWS] + acc[MROWS:]
                twice = jnp.concatenate([onehot[...], onehot[...]], axis=0).astype(BF16)
                total = None
                for part in split3(slot_grad):
                    one = mm(part.astype(BF16), twice)
                    total = one if total is None else total + one
                for stage in range(3):
                    grads[it, stage, places[stage]] = total
                    count = len(groups[stage])
                    for d in range(count):
                        grad_copy(it, stage, d).start()
                    for d in range(count):
                        grad_copy(it, stage, d).wait()
                    total = grads[it, stage, 0]
                    for d in range(count):
                        total = total + grads[it, stage, d + 1]
                mean = jnp.sum(total * total) * (1.0 / (128.0 * 36.0))
                coef[...] = coef[...] - STEP * total / jnp.sqrt(jnp.full(total.shape, mean + EPS, F32))

        lefts, _ = adjoint_lanes(cot[0] * (0.25 / NPIX), cot[1] * (0.25 / NPIX), t2.at[3])
        objects[s] = lanes_mul(lefts[0], t1.at[2])
        for d in range(3):
            gather_copy(d).start()
        for d in range(3):
            gather_copy(d).wait()

        for d in range(2):
            near_copy(d).wait()
        for d in range(2):
            wanted = near[1 - d]
            total = None
            for p in range(4):
                match = jnp.where(wanted == 4 * t + p, 1.0, 0.0)
                one = jnp.max(match[:1, :], axis=1, keepdims=True) * objects[p]
                total = one if total is None else total + one
            send[d] = total
            object_copy(d).start()
        for d in range(2):
            object_copy(d).wait()
        for j in range(4):
            source = incoming[j]
            total = jnp.where(source // 4 == (t + 31) % 32, arrive[0], arrive[1])
            for p in range(4):
                total = jnp.where(source == 4 * t + p, objects[p], total)
            out[j] = total
        coef_out[...] = coef[0:36, :]

    return kernel


def per_device(observed, frame_pick, frame_count, incoming, start_coefficients, mode_basis):
    tables, mask, weight, flip = host_tables()
    vmem = pl.BlockSpec(memory_space=pltpu.VMEM)
    smem = pl.BlockSpec(memory_space=pltpu.SMEM)
    hbm = pl.BlockSpec(memory_space=pl.ANY)
    dma = pltpu.SemaphoreType.DMA
    objects, coef = pl.pallas_call(
        make_kernel(),
        out_shape=(
            jax.ShapeDtypeStruct((4, NPIX, NPIX), F32),
            jax.ShapeDtypeStruct((36, 128), F32),
        ),
        in_specs=[hbm, hbm, smem, smem, vmem, smem, vmem, vmem, vmem] + [hbm] * 6,
        out_specs=(vmem, vmem),
        scratch_shapes=[
            pltpu.VMEM((4, 8, NPIX, NPIX), BF16),
            pltpu.VMEM((MROWS * XN, NPIX), F32),
            pltpu.VMEM((4, 8, 128), jnp.int32),
            pltpu.VMEM((4, 8, 128), jnp.int32),
            pltpu.VMEM((FR, 128), F32),
            pltpu.VMEM((8, 256), F32),
            pltpu.VMEM((MROWS, 128), F32),
            pltpu.VMEM((8, 128), jnp.int32),
            pltpu.VMEM((4, 256, 256), BF16),
            pltpu.VMEM((4, 128, 384), BF16),
            pltpu.VMEM((128, 224), BF16),
            pltpu.VMEM((80, 384), BF16),
            pltpu.VMEM((384, 256), BF16),
            pltpu.VMEM((256, 256), BF16),
            pltpu.VMEM((QUADS, 256, 256), F32),
            pltpu.VMEM((TILES, 256, 256), BF16),
            pltpu.VMEM((FR, 256), BF16),
            pltpu.VMEM((40 * FR, 128), F32),
            pltpu.VMEM((40 * FR, 128), F32),
            pltpu.VMEM((FR, XN, 128), F32),
            pltpu.VMEM((2 * QUADS, 256, 256), F32),
            pltpu.VMEM((QUADS, 256, 256), F32),
            pltpu.VMEM((3, 128, 128), F32),
            pltpu.VMEM((ITERS, 3, 8, MROWS, 128), F32),
            pltpu.VMEM((4, 128, 128), F32),
            pltpu.VMEM((2, 8, 128), jnp.int32),
            pltpu.VMEM((2, 128, 128), F32),
            pltpu.VMEM((2, 128, 128), F32),
            dma((3,)),
            dma((3,)),
            dma((3,)),
            dma((3,)),
            dma((ITERS, 3, 7)),
            dma((ITERS, 3, 7)),
            dma((3,)),
            dma((3,)),
            dma((2, 2)),
            dma((2, 2)),
            dma((36,)),
            dma((7,)),
        ],
        compiler_params=pltpu.CompilerParams(
            collective_id=0, has_side_effects=True, vmem_limit_bytes=56 * 1024 * 1024
        ),
        cost_estimate=pl.CostEstimate(flops=30_000_000_000, bytes_accessed=10_000_000, transcendentals=0),
    )(
        observed, mode_basis, frame_pick, frame_count, start_coefficients.T, incoming,
        *[jnp.asarray(one) for one in [mask, weight, flip] + tables],
    )
    return objects, coef.T


def solution(mesh):
    placed = (P("tile", "spare", None, None), P("tile", "spare"), P("tile"), P("tile"), P(), P())
    return jax.shard_map(
        per_device,
        mesh=mesh,
        in_specs=placed,
        out_specs=(P("tile", None, None), P()),
        check_vma=False,
    )
```

time: 113 us -> 89.8 us (0.79)
  Pallas kernels: 109 us -> 86 us
    pallas_call x1, Pallas kernels: 109 us -> 86 us  [per_device(): pl.pallas_call(make_kernel(), out_shape=(jax.ShapeDtypeStruct((4, NPIX, N...]
where the time goes in v2:
time: 89.8 us; the launch traced here: 89.6 us
  Pallas kernels  86 us (96%)
  local copies, waits for them, and re-layouts  3 us (3%)
    pallas_call x1, Pallas kernels, per_device(): pl.pallas_call(make_kernel(), out_shape=(jax.ShapeDtypeStruct((4, NPIX, N...  86 us
    unnamed x2, local copies, waits for them, and re-layouts  3 us

profile of v2, /device:TPU:1, one launch (start us, length us, event | category | flops | bytes accessed | tf_op | source)
XLA Modules:
  0.0 89.6 jit_solution(12178230991624229840)
XLA Ops:
  0.6 86.0 %shard_map.158 = (f32[4,128,128]{2,1,0:T(8,128)}, f32[36,128]{1,0:T(8,128)}) custom-call(bf16[4,8,128,128]{3,2,1,0:T(8,128)(2,1)} %observed_h.1, f32[36,128,128]{2,1,0:T(8,128)} %basis_h.1, s32[4,8]{1,0:T(4,128)} %pick.1, s32[4]{0:T(128)} %count.1, f32[36,128]{1,0:T(8,128)} %bitcast.3, s32[4]{0:T(128)} %incoming.1, f32[72,128]{1,0:T(8,128)} %constant.18.clone.mask, ...), custom_call_target="tpu_custom_call" | custom-call | flops 30000001024 | bytes 10000000 | tf_op jit(solution)/shard_map/pallas_call | solution.py:546
  86.6 1.7 %copy.19 = f32[4,128,128]{2,1,0:T(8,128)} copy(f32[4,128,128]{2,1,0:T(8,128)} %get-tuple-element.8) | data formatting | bytes 524288
  88.3 1.3 %copy.20 = f32[128,36]{0,1:T(8,128)} copy(f32[128,36]{0,1:T(8,128)} %bitcast.2) | data formatting | bytes 36864

commit v3 on v2

--- a/solution.py
+++ b/solution.py
@@ -21,7 +21,7 @@
 MROWS = 40
 FR = 32
 QUADS = 8
-PAIRS = 4
+PAIRS = 8
 STEPS = 16 // PAIRS
 TILES = 17
 

time: 89.8 us -> 84.9 us (0.945)
  Pallas kernels: 86 us -> 81 us
    pallas_call x1, Pallas kernels: 86 us -> 81 us  [per_device(): pl.pallas_call(make_kernel(), out_shape=(jax.ShapeDtypeStruct((4, NPIX, N...]
where the time goes in v3:
time: 84.9 us; the launch traced here: 84.7 us
  Pallas kernels  81 us (95%)
  local copies, waits for them, and re-layouts  3 us (4%)
    pallas_call x1, Pallas kernels, per_device(): pl.pallas_call(make_kernel(), out_shape=(jax.ShapeDtypeStruct((4, NPIX, N...  81 us
    unnamed x2, local copies, waits for them, and re-layouts  3 us

profile of v3, /device:TPU:1, one launch (start us, length us, event | category | flops | bytes accessed | tf_op | source)
XLA Modules:
  0.0 84.7 jit_solution(9848752180890790258)
XLA Ops:
  0.6 81.0 %shard_map.158 = (f32[4,128,128]{2,1,0:T(8,128)}, f32[36,128]{1,0:T(8,128)}) custom-call(bf16[4,8,128,128]{3,2,1,0:T(8,128)(2,1)} %observed_h.1, f32[36,128,128]{2,1,0:T(8,128)} %basis_h.1, s32[4,8]{1,0:T(4,128)} %pick.1, s32[4]{0:T(128)} %count.1, f32[36,128]{1,0:T(8,128)} %bitcast.3, s32[4]{0:T(128)} %incoming.1, f32[72,128]{1,0:T(8,128)} %constant.18.clone.mask, ...), custom_call_target="tpu_custom_call" | custom-call | flops 30000001024 | bytes 10000000 | tf_op jit(solution)/shard_map/pallas_call | solution.py:546
  81.7 1.7 %copy.19 = f32[4,128,128]{2,1,0:T(8,128)} copy(f32[4,128,128]{2,1,0:T(8,128)} %get-tuple-element.8) | data formatting | bytes 524288
  83.3 1.3 %copy.20 = f32[128,36]{0,1:T(8,128)} copy(f32[128,36]{0,1:T(8,128)} %bitcast.2) | data formatting | bytes 36864

commit v4 on v3

--- a/solution.py
+++ b/solution.py
@@ -21,7 +21,7 @@
 MROWS = 40
 FR = 32
 QUADS = 8
-PAIRS = 8
+PAIRS = 16
 STEPS = 16 // PAIRS
 TILES = 17
 
@@ -470,7 +470,7 @@
             six[...] = coef_six(coef, onehot)
             phases(six, basis6, phi)
 
-            pl.loop(0, STEPS)(lambda h: forward(h, phi, mask, flip, w1, a2, t1, t2.at[0], field, amp, trans))
+            forward(0, phi, mask, flip, w1, a2, t1, t2.at[0], field, amp, trans)
 
             @pl.when(it == 0)
             def _():
@@ -479,13 +479,11 @@
                     frames_copy(d).wait()
                     prep_spectra((s + 3 - d) % 4, observed, t1, t2.at[2], spec)
 
-            pl.loop(0, 8)(lambda r: products(r, trans, spec, used, weight, cot))
+            pl.loop(0, 8, unroll=2)(lambda r: products(r, trans, spec, used, weight, cot))
 
             @pl.when(it < ITERS)
             def _():
-                pl.loop(0, STEPS)(
-                    lambda h: backward(h, cot, spec, trans, used, flip, t2.at[1], t1, a2t, w1t, amp, field, dphi)
-                )
+                backward(0, cot, spec, trans, used, flip, t2.at[1], t1, a2t, w1t, amp, field, dphi)
                 acc = modes(dphi, basis6)
                 slot_grad = acc[:MROWS] + acc[MROWS:]
                 twice = jnp.concatenate([onehot[...], onehot[...]], axis=0).astype(BF16)

time: 84.9 us -> 82.6 us (0.973)
  Pallas kernels: 81 us -> 78.7 us
    pallas_call x1, Pallas kernels: 81 us -> 78.7 us  [per_device(): pl.pallas_call(make_kernel(), out_shape=(jax.ShapeDtypeStruct((4, NPIX, N...]
where the time goes in v4:
time: 82.6 us; the launch traced here: 82.3 us
  Pallas kernels  78.7 us (95%)
  local copies, waits for them, and re-layouts  3 us (4%)
    pallas_call x1, Pallas kernels, per_device(): pl.pallas_call(make_kernel(), out_shape=(jax.ShapeDtypeStruct((4, NPIX, N...  78.7 us
    unnamed x2, local copies, waits for them, and re-layouts  3 us

profile of v4, /device:TPU:1, one launch (start us, length us, event | category | flops | bytes accessed | tf_op | source)
XLA Modules:
  0.0 82.3 jit_solution(534454837028096154)
XLA Ops:
  0.6 78.7 %shard_map.158 = (f32[4,128,128]{2,1,0:T(8,128)}, f32[36,128]{1,0:T(8,128)}) custom-call(bf16[4,8,128,128]{3,2,1,0:T(8,128)(2,1)} %observed_h.1, f32[36,128,128]{2,1,0:T(8,128)} %basis_h.1, s32[4,8]{1,0:T(4,128)} %pick.1, s32[4]{0:T(128)} %count.1, f32[36,128]{1,0:T(8,128)} %bitcast.3, s32[4]{0:T(128)} %incoming.1, f32[72,128]{1,0:T(8,128)} %constant.18.clone.mask, ...), custom_call_target="tpu_custom_call" | custom-call | flops 30000001024 | bytes 10000000 | tf_op jit(solution)/shard_map/pallas_call | solution.py:544
  79.3 1.7 %copy.19 = f32[4,128,128]{2,1,0:T(8,128)} copy(f32[4,128,128]{2,1,0:T(8,128)} %get-tuple-element.8) | data formatting | bytes 524288
  81.0 1.3 %copy.20 = f32[128,36]{0,1:T(8,128)} copy(f32[128,36]{0,1:T(8,128)} %bitcast.2) | data formatting | bytes 36864

commit v5 on v4

--- a/solution.py
+++ b/solution.py
@@ -20,6 +20,8 @@
 X0, XN = 32, 72
 MROWS = 40
 FR = 32
+ODD = 33
+BODD = 73
 QUADS = 8
 PAIRS = 16
 STEPS = 16 // PAIRS
@@ -235,10 +237,10 @@
         halves = []
         for j in range(2):
             if last:
-                rows = pltpu.roll(basis[pl.ds(64 - 32 * j, MROWS, stride=XN), :], 96 - 64 * j, 1)
+                rows = pltpu.roll(basis[pl.ds(64 - 32 * j, MROWS, stride=BODD), :], 96 - 64 * j, 1)
             else:
-                one = pltpu.roll(basis[pl.ds(2 * i + j, MROWS, stride=XN), :], 96, 1)
-                other = pltpu.roll(basis[pl.ds(2 * i + j + 32, MROWS, stride=XN), :], 32, 1)
+                one = pltpu.roll(basis[pl.ds(2 * i + j, MROWS, stride=BODD), :], 96, 1)
+                other = pltpu.roll(basis[pl.ds(2 * i + j + 32, MROWS, stride=BODD), :], 32, 1)
                 rows = jnp.where(lane < 64, one, other)
             high, mid, low = split3(rows)
             halves.append(
@@ -254,12 +256,12 @@
     def phases(six, basis6, phi):
         for i in range(TILES):
             both = mm(six[...], basis6[i])
-            phi[pl.ds(2 * i * FR, FR), :] = both[:, :128]
-            phi[pl.ds((2 * i + 1) * FR, FR), :] = both[:, 128:]
+            phi[pl.ds(2 * i * ODD, FR), :] = both[:, :128]
+            phi[pl.ds((2 * i + 1) * ODD, FR), :] = both[:, 128:]
 
     def frame_field(f, phi, mask):
         lane = lax.broadcasted_iota(jnp.int32, (8, 128), 1)[:1]
-        packed = phi[pl.ds(f, 40, stride=FR), :]
+        packed = phi[pl.ds(f, 40, stride=ODD), :]
         turned = pltpu.roll(packed, 64, 1)
         phase = jnp.concatenate(
             [jnp.where(lane < 64, packed, turned), jnp.where(lane < 64, turned[:32], packed[:32])], axis=0
@@ -270,8 +272,8 @@
     def modes(dphi, basis6):
         total = None
         for i in range(TILES):
-            a = dphi[pl.ds(2 * i * FR, FR), :]
-            b = dphi[pl.ds((2 * i + 1) * FR, FR), :]
+            a = dphi[pl.ds(2 * i * ODD, FR), :]
+            b = dphi[pl.ds((2 * i + 1) * ODD, FR), :]
             high, low = split(jnp.concatenate([a, b], axis=1))
             part = mm_nt(basis6[i, 0 : 2 * MROWS, :], jnp.concatenate([high, low], axis=0))
             total = part if total is None else total + part
@@ -360,7 +362,7 @@
                 f, place = 2 * (PAIRS * h + i) + half, 2 * i + half
                 v = field[f] * d[XN * place : XN * place + XN]
                 v = v + pltpu.roll(v, 64, 1)
-                dphi[pl.ds(f, 40, stride=FR), :] = jnp.concatenate(
+                dphi[pl.ds(f, 40, stride=ODD), :] = jnp.concatenate(
                     [jnp.where(lane < 64, v[:32], v[32:64]), jnp.where(lane < 64, v[64:], 0.0)], axis=0
                 )
 
@@ -368,7 +370,7 @@
         observed_h, basis_h, pick, count, coef0, incoming, mask, weight, flip,
         t1_h, t2_h, a2_h, a2t_h, w1_h, w1t_h,
         out, coef_out,
-        observed, basis, picks, picked, onehot, used, coef, own, t1, t2, a2, a2t, w1, w1t,
+        observed, window, basis, picks, picked, onehot, used, coef, own, t1, t2, a2, a2t, w1, w1t,
         spec, basis6, six, phi, dphi, field, amp, trans, cot, grads, objects, near, send, arrive,
         ob_send, ob_recv, pk_send, pk_recv, gr_send, gr_recv, ag_send, ag_recv, nb_send, nb_recv, basis_sem, load_sem,
     ):
@@ -396,7 +398,7 @@
         ]
         windows = [
             pltpu.make_async_copy(
-                basis_h.at[m, pl.ds(X0, XN), :], basis.at[pl.ds(m * XN, XN), :], basis_sem.at[m]
+                basis_h.at[m, pl.ds(X0, XN), :], window.at[m], basis_sem.at[m]
             )
             for m in range(36)
         ]
@@ -452,10 +454,11 @@
         used[...] = jnp.where(4 * (4 * (row2 % 2) + lane2 // 64) + row2 // 2 < count[s], 1.0, 0.0)
         coef[...] = jnp.zeros_like(coef)
         coef[0:36, :] = coef0[...]
-        basis[pl.ds(36 * XN, 4 * XN), :] = jnp.zeros((4 * XN, NPIX), F32)
-        phi[pl.ds(2 * TILES * FR, 6 * FR), :] = jnp.zeros((6 * FR, 128), F32)
-        for one in windows:
-            one.wait()
+        basis[pl.ds(36 * BODD, 4 * BODD), :] = jnp.zeros((4 * BODD, NPIX), F32)
+        phi[...] = jnp.zeros_like(phi)
+        for m in range(36):
+            windows[m].wait()
+            basis[pl.ds(m * BODD, XN), :] = window[m]
         pl.loop(0, TILES - 1)(lambda i: prep_basis(i, basis, basis6))
         prep_basis(TILES - 1, basis, basis6, last=True)
         for d in range(3):
@@ -551,7 +554,8 @@
         out_specs=(vmem, vmem),
         scratch_shapes=[
             pltpu.VMEM((4, 8, NPIX, NPIX), BF16),
-            pltpu.VMEM((MROWS * XN, NPIX), F32),
+            pltpu.VMEM((36, XN, NPIX), F32),
+            pltpu.VMEM((MROWS * BODD, NPIX), F32),
             pltpu.VMEM((4, 8, 128), jnp.int32),
             pltpu.VMEM((4, 8, 128), jnp.int32),
             pltpu.VMEM((FR, 128), F32),
@@ -567,8 +571,8 @@
             pltpu.VMEM((QUADS, 256, 256), F32),
             pltpu.VMEM((TILES, 256, 256), BF16),
             pltpu.VMEM((FR, 256), BF16),
-            pltpu.VMEM((40 * FR, 128), F32),
-            pltpu.VMEM((40 * FR, 128), F32),
+            pltpu.VMEM((40 * ODD, 128), F32),
+            pltpu.VMEM((40 * ODD, 128), F32),
             pltpu.VMEM((FR, XN, 128), F32),
             pltpu.VMEM((2 * QUADS, 256, 256), F32),
             pltpu.VMEM((QUADS, 256, 256), F32),

time: 82.6 us -> 81.5 us (0.987)
  Pallas kernels: 78.7 us -> 77.6 us
    pallas_call x1, Pallas kernels: 78.7 us -> 77.6 us  [per_device(): pl.pallas_call(make_kernel(), out_shape=(jax.ShapeDtypeStruct((4, NPIX, N...]
where the time goes in v5:
time: 81.5 us; the launch traced here: 81.3 us
  Pallas kernels  77.6 us (95%)
  local copies, waits for them, and re-layouts  3 us (4%)
    pallas_call x1, Pallas kernels, per_device(): pl.pallas_call(make_kernel(), out_shape=(jax.ShapeDtypeStruct((4, NPIX, N...  77.6 us
    unnamed x2, local copies, waits for them, and re-layouts  3 us

profile of v5, /device:TPU:1, one launch (start us, length us, event | category | flops | bytes accessed | tf_op | source)
XLA Modules:
  0.0 81.3 jit_solution(2695753992536602671)
XLA Ops:
  0.6 77.6 %shard_map.158 = (f32[4,128,128]{2,1,0:T(8,128)}, f32[36,128]{1,0:T(8,128)}) custom-call(bf16[4,8,128,128]{3,2,1,0:T(8,128)(2,1)} %observed_h.1, f32[36,128,128]{2,1,0:T(8,128)} %basis_h.1, s32[4,8]{1,0:T(4,128)} %pick.1, s32[4]{0:T(128)} %count.1, f32[36,128]{1,0:T(8,128)} %bitcast.3, s32[4]{0:T(128)} %incoming.1, f32[72,128]{1,0:T(8,128)} %constant.18.clone.mask, ...), custom_call_target="tpu_custom_call" | custom-call | flops 30000001024 | bytes 10000000 | tf_op jit(solution)/shard_map/pallas_call | solution.py:547
  78.3 1.7 %copy.19 = f32[4,128,128]{2,1,0:T(8,128)} copy(f32[4,128,128]{2,1,0:T(8,128)} %get-tuple-element.8) | data formatting | bytes 524288
  79.9 1.3 %copy.20 = f32[128,36]{0,1:T(8,128)} copy(f32[128,36]{0,1:T(8,128)} %bitcast.2) | data formatting | bytes 36864

commit v6 on v5

--- a/solution.py
+++ b/solution.py
@@ -24,7 +24,6 @@
 BODD = 73
 QUADS = 8
 PAIRS = 16
-STEPS = 16 // PAIRS
 TILES = 17
 
 
@@ -153,7 +152,7 @@
     )
 
 
-COS_POLY = (1.0, -4.93480214, 4.05870915, -1.33521195, 0.23493707, -0.02439593)
+COS_POLY = (0.9999999889, -19.7392044666, 64.9391159283, -85.4501134275, 60.1674297919, -25.9668846126, 6.5277059630)
 
 
 def horner(poly, z):
@@ -163,11 +162,9 @@
     return total
 
 
-def unit_field(half_turns, mask):
-    k = jnp.floor(half_turns + 0.5)
-    r = half_turns - k
-    signed = mask * (1.0 - 2.0 * k + 4.0 * jnp.floor(0.5 * k))
-    return signed * horner(COS_POLY, r * r)
+def unit_field(turns, mask):
+    r = turns - jnp.floor(turns + 0.5)
+    return mask * horner(COS_POLY, r * r)
 
 
 def lane_mask(width, first):
@@ -222,15 +219,19 @@
 
 
 def make_kernel():
-    def prep_spectra(source, observed, t1, t2, spec):
-        sides = []
-        for half in range(2):
-            both = [mm(observed[source, 2 * i + half], t1[half, 0:128, :]) for i in range(4)]
-            sides.append([(one[:, :128] + one[:, 128:]) * (1.0 / NPIX) for one in both])
-        for j in range(2):
-            real, imag = half_spectra(sides[0][2 * j : 2 * j + 2], sides[1][2 * j : 2 * j + 2], t2)
-            spec[2 * source + j, :128, :] = real
-            spec[2 * source + j, 128:, :] = imag
+    def prep_spectra(sources, observed, t1, t2, spec):
+        lanes = []
+        for source in sources:
+            sides = []
+            for half in range(2):
+                both = [mm(observed[source, 2 * i + half], t1[half, 0:128, :]) for i in range(4)]
+                sides.append([(one[:, :128] + one[:, 128:]) * (1.0 / NPIX) for one in both])
+            lanes.append(sides)
+        for source, sides in zip(sources, lanes):
+            for j in range(2):
+                real, imag = half_spectra(sides[0][2 * j : 2 * j + 2], sides[1][2 * j : 2 * j + 2], t2)
+                spec[2 * source + j, :128, :] = real
+                spec[2 * source + j, 128:, :] = imag
 
     def prep_basis(i, basis, basis6, last=False):
         lane = lax.broadcasted_iota(jnp.int32, (MROWS, 128), 1)
@@ -249,7 +250,7 @@
         basis6[i] = jnp.concatenate(halves, axis=1).astype(BF16)
 
     def coef_six(coef, onehot):
-        high, mid, low = split3(coef[...] * (1.0 / math.pi))
+        high, mid, low = split3(coef[...] * (0.5 / math.pi))
         stack = jnp.concatenate([high, high, mid, high, mid, low, jnp.zeros((16, NPIX), F32)], axis=0)
         return mm_nt(onehot[...].astype(BF16), stack.astype(BF16)).astype(BF16)
 
@@ -267,7 +268,7 @@
             [jnp.where(lane < 64, packed, turned), jnp.where(lane < 64, turned[:32], packed[:32])], axis=0
         )
         phase = jnp.concatenate([phase[:32], phase[40:], phase[32:40]], axis=0)
-        return unit_field(phase - jnp.where(lane < 64, 0.0, 0.5), mask[...])
+        return unit_field(phase - jnp.where(lane < 64, 0.0, 0.25), mask[...])
 
     def modes(dphi, basis6):
         total = None
@@ -279,13 +280,14 @@
             total = part if total is None else total + part
         return total
 
-    def forward(h, phi, mask, flip, w1, a2, t1, t2, field, amp, trans):
+    def forward(phi, mask, flip, w1, a2, t1, t2, field, amp, trans, keep):
         stack = []
         for i in range(PAIRS):
             for half in range(2):
-                f = 2 * (PAIRS * h + i) + half
+                f = 2 * i + half
                 one = frame_field(f, phi, mask)
-                field[f] = one
+                if keep:
+                    field[f] = one
                 stack.append(one)
         b = right_mul(jnp.concatenate(stack, axis=0), w1)
         spreads = [[], []]
@@ -298,15 +300,15 @@
                 left_pupil(a2, jnp.concatenate([parts[0][:, :128], parts[1][:, :128]], axis=1)),
                 left_pupil(a2, jnp.concatenate([parts[0][:, 128:], parts[1][:, 128:]], axis=1)),
             )
-            amp[PAIRS * h + i, :128, :] = ar
-            amp[PAIRS * h + i, 128:, :] = ai
+            if keep:
+                amp[i, :128, :] = ar
+                amp[i, 128:, :] = ai
             spread = ar * ar + ai * ai
             for half in range(2):
                 spreads[half].append(spread[:, 128 * half : 128 * half + 128])
         d = [lanes_mul(jnp.concatenate(spreads[half], axis=0), t1.at[half]) for half in range(2)]
-        for j in range(PAIRS // 2):
-            g = PAIRS // 2 * h + j
-            tr, ti = half_spectra(*[[rows_of(d[half], 2 * j), rows_of(d[half], 2 * j + 1)] for half in range(2)], t2)
+        for g in range(QUADS):
+            tr, ti = half_spectra(*[[rows_of(d[half], 2 * g), rows_of(d[half], 2 * g + 1)] for half in range(2)], t2)
             trans[g, :128, :] = tr
             trans[g, 128:, :] = ti
 
@@ -330,12 +332,11 @@
         cot[1, upper, :] = w * qi
         cot[2, upper, :] = w * (qr * qr + qi * qi)
 
-    def backward(h, cot, spec, trans, used, flip, t2t, t1, a2t, w1t, amp, field, dphi):
+    def backward(cot, spec, trans, used, flip, t2t, t1, a2t, w1t, amp, field, dphi):
         qr, qi, qq = [jnp.concatenate([cot[n], cot[n]], axis=1) for n in range(3)]
         sides = [[], []]
-        for j in range(PAIRS // 2):
-            g = PAIRS // 2 * h + j
-            u = used[pl.ds(g, 1), :]
+        for g in range(QUADS):
+            u = used[g : g + 1, :]
             tr, ti = trans[g, :128, :], trans[g, 128:, :]
             sr, si = spec[g, :128, :], spec[g, 128:, :]
             gr = u * (qq * tr - qr * sr - qi * si)
@@ -346,7 +347,7 @@
         stack = []
         for i in range(PAIRS):
             one = jnp.concatenate([rows_of(ds[0], i), rows_of(ds[1], i)], axis=1)
-            xr, xi = fold(amp[PAIRS * h + i, :128, :] * one, amp[PAIRS * h + i, 128:, :] * one)
+            xr, xi = fold(amp[i, :128, :] * one, amp[i, 128:, :] * one)
             dbr, dbi = left_mul(a2t, xr), left_mul(a2t, xi)
             for half in range(2):
                 cols = slice(128 * half, 128 * half + 128)
@@ -359,7 +360,7 @@
         lane = lax.broadcasted_iota(jnp.int32, (8, 128), 1)[:1]
         for i in range(PAIRS):
             for half in range(2):
-                f, place = 2 * (PAIRS * h + i) + half, 2 * i + half
+                f = place = 2 * i + half
                 v = field[f] * d[XN * place : XN * place + XN]
                 v = v + pltpu.roll(v, 64, 1)
                 dphi[pl.ds(f, 40, stride=ODD), :] = jnp.concatenate(
@@ -459,8 +460,8 @@
         for m in range(36):
             windows[m].wait()
             basis[pl.ds(m * BODD, XN), :] = window[m]
-        pl.loop(0, TILES - 1)(lambda i: prep_basis(i, basis, basis6))
-        prep_basis(TILES - 1, basis, basis6, last=True)
+        for i in range(TILES):
+            prep_basis(i, basis, basis6, last=i == TILES - 1)
         for d in range(3):
             picks_copy(d).wait()
         for a in range(4):
@@ -468,45 +469,50 @@
         for one in loads:
             one.wait()
 
-        @pl.loop(0, ITERS + 1)
-        def iteration(it):
+        def transfer(keep):
             six[...] = coef_six(coef, onehot)
             phases(six, basis6, phi)
-
-            forward(0, phi, mask, flip, w1, a2, t1, t2.at[0], field, amp, trans)
+            forward(phi, mask, flip, w1, a2, t1, t2.at[0], field, amp, trans, keep)
+
+        def ratios():
+            pl.loop(0, 8, unroll=2)(lambda r: products(r, trans, spec, used, weight, cot))
+
+        @pl.loop(0, ITERS)
+        def iteration(it):
+            transfer(keep=True)
 
             @pl.when(it == 0)
             def _():
-                prep_spectra(s, observed, t1, t2.at[2], spec)
-                for d in (0, 2, 1):
-                    frames_copy(d).wait()
-                    prep_spectra((s + 3 - d) % 4, observed, t1, t2.at[2], spec)
-
-            pl.loop(0, 8, unroll=2)(lambda r: products(r, trans, spec, used, weight, cot))
-
-            @pl.when(it < ITERS)
-            def _():
-                backward(0, cot, spec, trans, used, flip, t2.at[1], t1, a2t, w1t, amp, field, dphi)
-                acc = modes(dphi, basis6)
-                slot_grad = acc[:MROWS] + acc[MROWS:]
-                twice = jnp.concatenate([onehot[...], onehot[...]], axis=0).astype(BF16)
-                total = None
-                for part in split3(slot_grad):
-                    one = mm(part.astype(BF16), twice)
-                    total = one if total is None else total + one
-                for stage in range(3):
-                    grads[it, stage, places[stage]] = total
-                    count = len(groups[stage])
-                    for d in range(count):
-                        grad_copy(it, stage, d).start()
-                    for d in range(count):
-                        grad_copy(it, stage, d).wait()
-                    total = grads[it, stage, 0]
-                    for d in range(count):
-                        total = total + grads[it, stage, d + 1]
-                mean = jnp.sum(total * total) * (1.0 / (128.0 * 36.0))
-                coef[...] = coef[...] - STEP * total / jnp.sqrt(jnp.full(total.shape, mean + EPS, F32))
-
+                frames_copy(0).wait()
+                frames_copy(2).wait()
+                prep_spectra([s, (s + 3) % 4, (s + 1) % 4], observed, t1, t2.at[2], spec)
+                frames_copy(1).wait()
+                prep_spectra([(s + 2) % 4], observed, t1, t2.at[2], spec)
+
+            ratios()
+            backward(cot, spec, trans, used, flip, t2.at[1], t1, a2t, w1t, amp, field, dphi)
+            acc = modes(dphi, basis6)
+            slot_grad = acc[:MROWS] + acc[MROWS:]
+            twice = jnp.concatenate([onehot[...], onehot[...]], axis=0).astype(BF16)
+            total = None
+            for part in split3(slot_grad):
+                one = mm(part.astype(BF16), twice)
+                total = one if total is None else total + one
+            for stage in range(3):
+                grads[it, stage, places[stage]] = total
+                count = len(groups[stage])
+                for d in range(count):
+                    grad_copy(it, stage, d).start()
+                for d in range(count):
+                    grad_copy(it, stage, d).wait()
+                total = grads[it, stage, 0]
+                for d in range(count):
+                    total = total + grads[it, stage, d + 1]
+            mean = jnp.sum(total * total) * (1.0 / (128.0 * 36.0))
+            coef[...] = coef[...] - STEP * total / jnp.sqrt(jnp.full(total.shape, mean + EPS, F32))
+
+        transfer(keep=False)
+        ratios()
         lefts, _ = adjoint_lanes(cot[0] * (0.25 / NPIX), cot[1] * (0.25 / NPIX), t2.at[3])
         objects[s] = lanes_mul(lefts[0], t1.at[2])
         for d in range(3):
@@ -536,6 +542,11 @@
         coef_out[...] = coef[0:36, :]
 
     return kernel
+
+
+def hand_on(objects, coef, out, coef_out):
+    out[...] = objects[...]
+    coef_out[...] = coef[...]
 
 
 def per_device(observed, frame_pick, frame_count, incoming, start_coefficients, mode_basis):
@@ -603,7 +614,14 @@
         observed, mode_basis, frame_pick, frame_count, start_coefficients.T, incoming,
         *[jnp.asarray(one) for one in [mask, weight, flip] + tables],
     )
-    return objects, coef.T
+    restored, coef = pl.pallas_call(
+        hand_on,
+        out_shape=(jax.ShapeDtypeStruct((4, NPIX, NPIX), F32), jax.ShapeDtypeStruct((36, 128), F32)),
+        in_specs=[vmem, vmem],
+        out_specs=(vmem, vmem),
+        cost_estimate=pl.CostEstimate(flops=500_000, bytes_accessed=700_000, transcendentals=0),
+    )(objects, coef)
+    return restored, coef.T
 
 
 def solution(mesh):

time: 81.5 us -> 79.8 us (0.979)
  local copies, waits for them, and re-layouts: 3 us -> 0 us
  Pallas kernels: 77.6 us -> 79 us
    unnamed x2 -> x0, local copies, waits for them, and re-layouts: 3 us -> none
    pallas_call x0 -> x1, Pallas kernels: none -> 1.68 us  [per_device(): pl.pallas_call(hand_on, out_shape=(jax.ShapeDtypeStruct((4, NPIX, NPIX),...]
where the time goes in v6:
time: 79.8 us; the launch traced here: 79.6 us
  Pallas kernels  79 us (99%)
    pallas_call x1, Pallas kernels, per_device(): pl.pallas_call(make_kernel(), out_shape=(jax.ShapeDtypeStruct((4, NPIX, N...  77.3 us
    pallas_call x1, Pallas kernels, per_device(): pl.pallas_call(hand_on, out_shape=(jax.ShapeDtypeStruct((4, NPIX, NPIX),...  1.68 us

profile of v6, /device:TPU:1, one launch (start us, length us, event | category | flops | bytes accessed | tf_op | source)
XLA Modules:
  0.0 79.6 jit_solution(17463736089792477949)
XLA Ops:
  0.6 77.3 %shard_map.158 = (f32[4,128,128]{2,1,0:T(8,128)}, f32[36,128]{1,0:T(8,128)}) custom-call(bf16[4,8,128,128]{3,2,1,0:T(8,128)(2,1)} %observed_h.1, f32[36,128,128]{2,1,0:T(8,128)} %basis_h.1, s32[4,8]{1,0:T(4,128)} %pick.1, s32[4]{0:T(128)} %count.1, f32[36,128]{1,0:T(8,128)} %bitcast.2, s32[4]{0:T(128)} %incoming.1, f32[72,128]{1,0:T(8,128)} %constant.18.clone.mask, ...), custom_call_target="tpu_custom_call" | custom-call | flops 30000001024 | bytes 10000000 | tf_op jit(solution)/shard_map/pallas_call | solution.py:558
  78.0 1.7 %shard_map.159 = (f32[4,128,128]{2,1,0:T(8,128)}, f32[36,128]{1,0:T(8,128)}) custom-call(f32[4,128,128]{2,1,0:T(8,128)} %get-tuple-element.6.objects, f32[36,128]{1,0:T(8,128)} %get-tuple-element.7.coef), custom_call_target="tpu_custom_call" | custom-call | flops 500000 | bytes 700000 | tf_op jit(solution)/shard_map/pallas_call | solution.py:617

commit v7 on v6

--- a/solution.py
+++ b/solution.py
@@ -371,7 +371,7 @@
         observed_h, basis_h, pick, count, coef0, incoming, mask, weight, flip,
         t1_h, t2_h, a2_h, a2t_h, w1_h, w1t_h,
         out, coef_out,
-        observed, window, basis, picks, picked, onehot, used, coef, own, t1, t2, a2, a2t, w1, w1t,
+        observed, relay, window, basis, picks, picked, onehot, used, coef, own, t1, t2, a2, a2t, w1, w1t,
         spec, basis6, six, phi, dphi, field, amp, trans, cot, grads, objects, near, send, arrive,
         ob_send, ob_recv, pk_send, pk_recv, gr_send, gr_recv, ag_send, ag_recv, nb_send, nb_recv, basis_sem, load_sem,
     ):
@@ -417,8 +417,24 @@
         def object_copy(d):
             return remote(send.at[d], arrive.at[d], nb_send.at[1, d], nb_recv.at[1, d], beside[d])
 
-        def frames_copy(d):
-            return remote(observed_h.at[spare_of[d]], observed.at[s], ob_send.at[d], ob_recv.at[d], groups[0][d])
+        ways = [(s + 1) % 4, (s + 3) % 4]
+        across = (s + 2) % 4
+
+        def frames_copy(way):
+            return remote(
+                observed_h.at[ways[way]], observed.at[s], ob_send.at[0, way], ob_recv.at[0, way], (t, ways[way])
+            )
+
+        def relay_copy(way):
+            return remote(
+                observed_h.at[across, pl.ds(4 * way, 4)], relay.at[way], ob_send.at[1, way], ob_recv.at[1, way], (t, ways[way])
+            )
+
+        def onward_copy(way):
+            return remote(
+                relay.at[way], observed.at[ways[1 - way], pl.ds(4 * way, 4)], ob_send.at[2, way], ob_recv.at[2, way],
+                (t, ways[way]),
+            )
 
         def picks_copy(d):
             return remote(picks.at[spare_of[d]], picked.at[s], pk_send.at[d], pk_recv.at[d], groups[0][d])
@@ -445,8 +461,10 @@
         pl.semaphore_wait(barrier, len(partners))
         for d in range(3):
             picks_copy(d).start()
-        for d in (1, 0, 2):
-            frames_copy(d).start()
+        for way in range(2):
+            relay_copy(way).start()
+        for way in range(2):
+            frames_copy(way).start()
         for d in range(2):
             near_copy(d).start()
 
@@ -469,9 +487,11 @@
         for one in loads:
             one.wait()
 
-        def transfer(keep):
+        def transfer(keep, between=None):
             six[...] = coef_six(coef, onehot)
             phases(six, basis6, phi)
+            if between is not None:
+                between()
             forward(phi, mask, flip, w1, a2, t1, t2.at[0], field, amp, trans, keep)
 
         def ratios():
@@ -479,15 +499,23 @@
 
         @pl.loop(0, ITERS)
         def iteration(it):
-            transfer(keep=True)
+            def pass_on():
+                @pl.when(it == 0)
+                def _():
+                    for way in range(2):
+                        relay_copy(way).wait()
+                        onward_copy(way).start()
+
+            transfer(keep=True, between=pass_on)
 
             @pl.when(it == 0)
             def _():
-                frames_copy(0).wait()
-                frames_copy(2).wait()
-                prep_spectra([s, (s + 3) % 4, (s + 1) % 4], observed, t1, t2.at[2], spec)
-                frames_copy(1).wait()
-                prep_spectra([(s + 2) % 4], observed, t1, t2.at[2], spec)
+                for way in range(2):
+                    frames_copy(way).wait()
+                prep_spectra([s] + ways, observed, t1, t2.at[2], spec)
+                for way in range(2):
+                    onward_copy(way).wait()
+                prep_spectra([across], observed, t1, t2.at[2], spec)
 
             ratios()
             backward(cot, spec, trans, used, flip, t2.at[1], t1, a2t, w1t, amp, field, dphi)
@@ -565,6 +593,7 @@
         out_specs=(vmem, vmem),
         scratch_shapes=[
             pltpu.VMEM((4, 8, NPIX, NPIX), BF16),
+            pltpu.VMEM((2, 4, NPIX, NPIX), BF16),
             pltpu.VMEM((36, XN, NPIX), F32),
             pltpu.VMEM((MROWS * BODD, NPIX), F32),
             pltpu.VMEM((4, 8, 128), jnp.int32),
@@ -593,8 +622,8 @@
             pltpu.VMEM((2, 8, 128), jnp.int32),
             pltpu.VMEM((2, 128, 128), F32),
             pltpu.VMEM((2, 128, 128), F32),
-            dma((3,)),
-            dma((3,)),
+            dma((3, 2)),
+            dma((3, 2)),
             dma((3,)),
             dma((3,)),
             dma((ITERS, 3, 7)),

time: 79.8 us -> 78.8 us (0.987)
  Pallas kernels: 79 us -> 77.9 us
    pallas_call x1, Pallas kernels: 77.3 us -> 76.3 us  [per_device(): pl.pallas_call(make_kernel(), out_shape=(jax.ShapeDtypeStruct((4, NPIX, N...]
where the time goes in v7:
time: 78.8 us; the launch traced here: 78.6 us
  Pallas kernels  77.9 us (99%)
    pallas_call x1, Pallas kernels, per_device(): pl.pallas_call(make_kernel(), out_shape=(jax.ShapeDtypeStruct((4, NPIX, N...  76.3 us
    pallas_call x1, Pallas kernels, per_device(): pl.pallas_call(hand_on, out_shape=(jax.ShapeDtypeStruct((4, NPIX, NPIX),...  1.68 us

profile of v7, /device:TPU:1, one launch (start us, length us, event | category | flops | bytes accessed | tf_op | source)
XLA Modules:
  0.0 78.6 jit_solution(18019580440760966422)
XLA Ops:
  0.6 76.3 %shard_map.158 = (f32[4,128,128]{2,1,0:T(8,128)}, f32[36,128]{1,0:T(8,128)}) custom-call(bf16[4,8,128,128]{3,2,1,0:T(8,128)(2,1)} %observed_h.1, f32[36,128,128]{2,1,0:T(8,128)} %basis_h.1, s32[4,8]{1,0:T(4,128)} %pick.1, s32[4]{0:T(128)} %count.1, f32[36,128]{1,0:T(8,128)} %bitcast.2, s32[4]{0:T(128)} %incoming.1, f32[72,128]{1,0:T(8,128)} %constant.18.clone.mask, ...), custom_call_target="tpu_custom_call" | custom-call | flops 30000001024 | bytes 10000000 | tf_op jit(solution)/shard_map/pallas_call | solution.py:586
  76.9 1.7 %shard_map.159 = (f32[4,128,128]{2,1,0:T(8,128)}, f32[36,128]{1,0:T(8,128)}) custom-call(f32[4,128,128]{2,1,0:T(8,128)} %get-tuple-element.6.objects, f32[36,128]{1,0:T(8,128)} %get-tuple-element.7.coef), custom_call_target="tpu_custom_call" | custom-call | flops 500000 | bytes 700000 | tf_op jit(solution)/shard_map/pallas_call | solution.py:646

commit v8 on v7

--- a/solution.py
+++ b/solution.py
@@ -372,7 +372,7 @@
         t1_h, t2_h, a2_h, a2t_h, w1_h, w1t_h,
         out, coef_out,
         observed, relay, window, basis, picks, picked, onehot, used, coef, own, t1, t2, a2, a2t, w1, w1t,
-        spec, basis6, six, phi, dphi, field, amp, trans, cot, grads, objects, near, send, arrive,
+        spec, basis6, six, phi, dphi, field, amp, trans, cot, pieces, grads, objects, near, send, arrive,
         ob_send, ob_recv, pk_send, pk_recv, gr_send, gr_recv, ag_send, ag_recv, nb_send, nb_recv, basis_sem, load_sem,
     ):
         t, s = lax.axis_index("tile"), lax.axis_index("spare")
@@ -383,7 +383,8 @@
             [(((tx + d) % 4) * 8 + tz * 2 + tc, s) for d in (1, 2, 3)],
             [(tx * 8 + ((tz + d) % 4) * 2 + tc, s) for d in (1, 2, 3)],
         ]
-        places = [tc * 4 + s, tx, tz]
+        place = tc * 4 + s
+        piece_of = [tc * 4 + v for v in spare_of] + [(1 - tc) * 4 + (s + d) % 4 for d in range(4)]
         beside = [((t + 1) % 32, s), ((t + 31) % 32, s)]
 
         barrier = pltpu.get_barrier_semaphore()
@@ -439,12 +440,21 @@
         def picks_copy(d):
             return remote(picks.at[spare_of[d]], picked.at[s], pk_send.at[d], pk_recv.at[d], groups[0][d])
 
-        def gather_copy(d):
-            return remote(objects.at[s], objects.at[s], ag_send.at[d], ag_recv.at[d], groups[0][d])
+        def gather_copy(part, way):
+            here = objects.at[s, pl.ds(64 * (way ^ part), 64), :]
+            return remote(here, here, ag_send.at[part, way], ag_recv.at[part, way], (t, ways[way]))
+
+        def gather_onward(way):
+            here = objects.at[ways[1 - way], pl.ds(64 * way, 64), :]
+            return remote(here, here, ag_send.at[2, way], ag_recv.at[2, way], (t, ways[way]))
+
+        stages = [groups[0], groups[1], groups[2], groups[0]]
+        places = [place, tx, tz, place]
 
         def grad_copy(it, stage, d):
             here = grads.at[it, stage, places[stage]]
-            return remote(here, here, gr_send.at[it, stage, d], gr_recv.at[it, stage, d], groups[stage][d])
+            src = pieces.at[it, piece_of[d]] if stage == 0 else here
+            return remote(src, here, gr_send.at[it, stage, d], gr_recv.at[it, stage, d], stages[stage][d])
 
         lane = lax.broadcasted_iota(jnp.int32, (8, 128), 1)
         row = lax.broadcasted_iota(jnp.int32, (8, 128), 0)
@@ -526,16 +536,22 @@
             for part in split3(slot_grad):
                 one = mm(part.astype(BF16), twice)
                 total = one if total is None else total + one
-            for stage in range(3):
-                grads[it, stage, places[stage]] = total
-                count = len(groups[stage])
+            for j in range(8):
+                pieces[it, j, 0:5, :] = total[5 * j : 5 * j + 5]
+                pieces[it, j, 5:8, :] = jnp.zeros((3, 128), F32)
+            piece = pieces[it, place]
+            for stage in range(4):
+                grads[it, stage, places[stage]] = piece
+                count = len(stages[stage])
                 for d in range(count):
                     grad_copy(it, stage, d).start()
                 for d in range(count):
                     grad_copy(it, stage, d).wait()
-                total = grads[it, stage, 0]
-                for d in range(count):
-                    total = total + grads[it, stage, d + 1]
+                if stage < 3:
+                    piece = grads[it, stage, 0]
+                    for d in range(count):
+                        piece = piece + grads[it, stage, d + 1]
+            total = jnp.concatenate([grads[it, 3, j][0:5] for j in range(8)], axis=0)
             mean = jnp.sum(total * total) * (1.0 / (128.0 * 36.0))
             coef[...] = coef[...] - STEP * total / jnp.sqrt(jnp.full(total.shape, mean + EPS, F32))
 
@@ -543,10 +559,16 @@
         ratios()
         lefts, _ = adjoint_lanes(cot[0] * (0.25 / NPIX), cot[1] * (0.25 / NPIX), t2.at[3])
         objects[s] = lanes_mul(lefts[0], t1.at[2])
-        for d in range(3):
-            gather_copy(d).start()
-        for d in range(3):
-            gather_copy(d).wait()
+        for part in range(2):
+            for way in range(2):
+                gather_copy(part, way).start()
+        for way in range(2):
+            gather_copy(0, way).wait()
+            gather_onward(way).start()
+        for way in range(2):
+            gather_copy(1, way).wait()
+        for way in range(2):
+            gather_onward(way).wait()
 
         for d in range(2):
             near_copy(d).wait()
@@ -617,7 +639,8 @@
             pltpu.VMEM((2 * QUADS, 256, 256), F32),
             pltpu.VMEM((QUADS, 256, 256), F32),
             pltpu.VMEM((3, 128, 128), F32),
-            pltpu.VMEM((ITERS, 3, 8, MROWS, 128), F32),
+            pltpu.VMEM((ITERS, 8, 8, 128), F32),
+            pltpu.VMEM((ITERS, 4, 8, 8, 128), F32),
             pltpu.VMEM((4, 128, 128), F32),
             pltpu.VMEM((2, 8, 128), jnp.int32),
             pltpu.VMEM((2, 128, 128), F32),
@@ -626,10 +649,10 @@
             dma((3, 2)),
             dma((3,)),
             dma((3,)),
-            dma((ITERS, 3, 7)),
-            dma((ITERS, 3, 7)),
-            dma((3,)),
-            dma((3,)),
+            dma((ITERS, 4, 7)),
+            dma((ITERS, 4, 7)),
+            dma((3, 2)),
+            dma((3, 2)),
             dma((2, 2)),
             dma((2, 2)),
             dma((36,)),

time: 78.8 us -> 85.6 us (1.086)
  Pallas kernels: 77.9 us -> 84.8 us
    pallas_call x1, Pallas kernels: 76.3 us -> 83.1 us  [per_device(): pl.pallas_call(make_kernel(), out_shape=(jax.ShapeDtypeStruct((4, NPIX, N...]
where the time goes in v8:
time: 85.6 us; the launch traced here: 85.4 us
  Pallas kernels  84.8 us (99%)
    pallas_call x1, Pallas kernels, per_device(): pl.pallas_call(make_kernel(), out_shape=(jax.ShapeDtypeStruct((4, NPIX, N...  83.1 us

profile of v8, /device:TPU:1, one launch (start us, length us, event | category | flops | bytes accessed | tf_op | source)
XLA Modules:
  0.0 85.4 jit_solution(14716733932818598782)
XLA Ops:
  0.6 83.1 %shard_map.158 = (f32[4,128,128]{2,1,0:T(8,128)}, f32[36,128]{1,0:T(8,128)}) custom-call(bf16[4,8,128,128]{3,2,1,0:T(8,128)(2,1)} %observed_h.1, f32[36,128,128]{2,1,0:T(8,128)} %basis_h.1, s32[4,8]{1,0:T(4,128)} %pick.1, s32[4]{0:T(128)} %count.1, f32[36,128]{1,0:T(8,128)} %bitcast.2, s32[4]{0:T(128)} %incoming.1, f32[72,128]{1,0:T(8,128)} %constant.18.clone.mask, ...), custom_call_target="tpu_custom_call" | custom-call | flops 30000001024 | bytes 10000000 | tf_op jit(solution)/shard_map/pallas_call | solution.py:608
  83.7 1.7 %shard_map.159 = (f32[4,128,128]{2,1,0:T(8,128)}, f32[36,128]{1,0:T(8,128)}) custom-call(f32[4,128,128]{2,1,0:T(8,128)} %get-tuple-element.6.objects, f32[36,128]{1,0:T(8,128)} %get-tuple-element.7.coef), custom_call_target="tpu_custom_call" | custom-call | flops 500000 | bytes 700000 | tf_op jit(solution)/shard_map/pallas_call | solution.py:669

commit v9 on v7

--- a/solution.py
+++ b/solution.py
@@ -24,6 +24,7 @@
 BODD = 73
 QUADS = 8
 PAIRS = 16
+CHUNKS = 4
 TILES = 17
 
 
@@ -218,6 +219,13 @@
     return x[128 * n : 128 * n + 128]
 
 
+def staggered(*stages):
+    for step in range(CHUNKS + len(stages) - 1):
+        for k, stage in enumerate(stages):
+            if 0 <= step - k < CHUNKS:
+                stage(step - k)
+
+
 def make_kernel():
     def prep_spectra(sources, observed, t1, t2, spec):
         lanes = []
@@ -281,36 +289,48 @@
         return total
 
     def forward(phi, mask, flip, w1, a2, t1, t2, field, amp, trans, keep):
-        stack = []
-        for i in range(PAIRS):
-            for half in range(2):
-                f = 2 * i + half
+        first, second, third = {}, {}, {}
+
+        def along_y(c):
+            stack = []
+            for f in range(8 * c, 8 * c + 8):
                 one = frame_field(f, phi, mask)
                 if keep:
                     field[f] = one
                 stack.append(one)
-        b = right_mul(jnp.concatenate(stack, axis=0), w1)
-        spreads = [[], []]
-        for i in range(PAIRS):
-            parts = []
-            for half in range(2):
-                one = b[XN * (2 * i + half) : XN * (2 * i + half + 1)]
-                parts.append(jnp.concatenate([one[:64], one[64:] * flip[...]], axis=0))
-            ar, ai = unfold(
-                left_pupil(a2, jnp.concatenate([parts[0][:, :128], parts[1][:, :128]], axis=1)),
-                left_pupil(a2, jnp.concatenate([parts[0][:, 128:], parts[1][:, 128:]], axis=1)),
-            )
-            if keep:
-                amp[i, :128, :] = ar
-                amp[i, 128:, :] = ai
-            spread = ar * ar + ai * ai
-            for half in range(2):
-                spreads[half].append(spread[:, 128 * half : 128 * half + 128])
-        d = [lanes_mul(jnp.concatenate(spreads[half], axis=0), t1.at[half]) for half in range(2)]
-        for g in range(QUADS):
-            tr, ti = half_spectra(*[[rows_of(d[half], 2 * g), rows_of(d[half], 2 * g + 1)] for half in range(2)], t2)
-            trans[g, :128, :] = tr
-            trans[g, 128:, :] = ti
+            first[c] = right_mul(jnp.concatenate(stack, axis=0), w1)
+
+        def along_x(c):
+            b, spreads = first.pop(c), [[], []]
+            for i in range(4):
+                parts = []
+                for half in range(2):
+                    one = b[XN * (2 * i + half) : XN * (2 * i + half + 1)]
+                    parts.append(jnp.concatenate([one[:64], one[64:] * flip[...]], axis=0))
+                ar, ai = unfold(
+                    left_pupil(a2, jnp.concatenate([parts[0][:, :128], parts[1][:, :128]], axis=1)),
+                    left_pupil(a2, jnp.concatenate([parts[0][:, 128:], parts[1][:, 128:]], axis=1)),
+                )
+                if keep:
+                    amp[4 * c + i, :128, :] = ar
+                    amp[4 * c + i, 128:, :] = ai
+                spread = ar * ar + ai * ai
+                for half in range(2):
+                    spreads[half].append(spread[:, 128 * half : 128 * half + 128])
+            second[c] = spreads
+
+        def lanes(c):
+            spreads = second.pop(c)
+            third[c] = [lanes_mul(jnp.concatenate(spreads[half], axis=0), t1.at[half]) for half in range(2)]
+
+        def rows(c):
+            d = third.pop(c)
+            for g in range(2):
+                tr, ti = half_spectra(*[[rows_of(d[half], 2 * g), rows_of(d[half], 2 * g + 1)] for half in range(2)], t2)
+                trans[2 * c + g, :128, :] = tr
+                trans[2 * c + g, 128:, :] = ti
+
+        staggered(along_y, along_x, lanes, rows)
 
     def products(r, trans, spec, used, weight, cot):
         nr = ni = de = None
@@ -334,38 +354,51 @@
 
     def backward(cot, spec, trans, used, flip, t2t, t1, a2t, w1t, amp, field, dphi):
         qr, qi, qq = [jnp.concatenate([cot[n], cot[n]], axis=1) for n in range(3)]
-        sides = [[], []]
-        for g in range(QUADS):
-            u = used[g : g + 1, :]
-            tr, ti = trans[g, :128, :], trans[g, 128:, :]
-            sr, si = spec[g, :128, :], spec[g, 128:, :]
-            gr = u * (qq * tr - qr * sr - qi * si)
-            gi = u * (qi * sr - qr * si + qq * ti)
-            for half, one in enumerate(adjoint_lanes(gr, gi, t2t)):
-                sides[half] += one
-        ds = [lanes_mul(jnp.concatenate(sides[half], axis=0), t1.at[2 + half]) for half in range(2)]
-        stack = []
-        for i in range(PAIRS):
-            one = jnp.concatenate([rows_of(ds[0], i), rows_of(ds[1], i)], axis=1)
-            xr, xi = fold(amp[i, :128, :] * one, amp[i, 128:, :] * one)
-            dbr, dbi = left_mul(a2t, xr), left_mul(a2t, xi)
-            for half in range(2):
-                cols = slice(128 * half, 128 * half + 128)
-                one = jnp.concatenate([dbr[:XN, cols], dbi[:XN, cols]], axis=1)
-                stack += [one[:64], one[64:] * flip[...]]
-        x = jnp.concatenate(stack, axis=0)
-        n = x.shape[0]
-        both = mm(jnp.concatenate(split(x), axis=0), w1t[...])
-        d = both[:n, :128] + both[:n, 128:] + both[n:, :128] + both[n:, 128:]
         lane = lax.broadcasted_iota(jnp.int32, (8, 128), 1)[:1]
-        for i in range(PAIRS):
-            for half in range(2):
-                f = place = 2 * i + half
+        first, second, third = {}, {}, {}
+
+        def rows(c):
+            sides = [[], []]
+            for g in (2 * c, 2 * c + 1):
+                u = used[g : g + 1, :]
+                tr, ti = trans[g, :128, :], trans[g, 128:, :]
+                sr, si = spec[g, :128, :], spec[g, 128:, :]
+                gr = u * (qq * tr - qr * sr - qi * si)
+                gi = u * (qi * sr - qr * si + qq * ti)
+                for half, one in enumerate(adjoint_lanes(gr, gi, t2t)):
+                    sides[half] += one
+            first[c] = sides
+
+        def lanes(c):
+            sides = first.pop(c)
+            second[c] = [lanes_mul(jnp.concatenate(sides[half], axis=0), t1.at[2 + half]) for half in range(2)]
+
+        def along_x(c):
+            ds, stack = second.pop(c), []
+            for i in range(4):
+                one = jnp.concatenate([rows_of(ds[0], i), rows_of(ds[1], i)], axis=1)
+                xr, xi = fold(amp[4 * c + i, :128, :] * one, amp[4 * c + i, 128:, :] * one)
+                dbr, dbi = left_mul(a2t, xr), left_mul(a2t, xi)
+                for half in range(2):
+                    cols = slice(128 * half, 128 * half + 128)
+                    one = jnp.concatenate([dbr[:XN, cols], dbi[:XN, cols]], axis=1)
+                    stack += [one[:64], one[64:] * flip[...]]
+            third[c] = stack
+
+        def along_y(c):
+            x = jnp.concatenate(third.pop(c), axis=0)
+            n = x.shape[0]
+            both = mm(jnp.concatenate(split(x), axis=0), w1t[...])
+            d = both[:n, :128] + both[:n, 128:] + both[n:, :128] + both[n:, 128:]
+            for place in range(8):
+                f = 8 * c + place
                 v = field[f] * d[XN * place : XN * place + XN]
                 v = v + pltpu.roll(v, 64, 1)
                 dphi[pl.ds(f, 40, stride=ODD), :] = jnp.concatenate(
                     [jnp.where(lane < 64, v[:32], v[32:64]), jnp.where(lane < 64, v[64:], 0.0)], axis=0
                 )
+
+        staggered(rows, lanes, along_x, along_y)
 
     def kernel(
         observed_h, basis_h, pick, count, coef0, incoming, mask, weight, flip,

time: 78.8 us -> 76.9 us (0.976)
  Pallas kernels: 77.9 us -> 76.1 us
    pallas_call x1, Pallas kernels: 76.3 us -> 74.4 us  [per_device(): pl.pallas_call(make_kernel(), out_shape=(jax.ShapeDtypeStruct((4, NPIX, N...]
where the time goes in v9:
time: 76.9 us; the launch traced here: 76.7 us
  Pallas kernels  76.1 us (99%)
    pallas_call x1, Pallas kernels, per_device(): pl.pallas_call(make_kernel(), out_shape=(jax.ShapeDtypeStruct((4, NPIX, N...  74.4 us
    pallas_call x1, Pallas kernels, per_device(): pl.pallas_call(hand_on, out_shape=(jax.ShapeDtypeStruct((4, NPIX, NPIX),...  1.68 us

profile of v9, /device:TPU:1, one launch (start us, length us, event | category | flops | bytes accessed | tf_op | source)
XLA Modules:
  0.0 76.7 jit_solution(12736519389834213298)
XLA Ops:
  0.6 74.4 %shard_map.158 = (f32[4,128,128]{2,1,0:T(8,128)}, f32[36,128]{1,0:T(8,128)}) custom-call(bf16[4,8,128,128]{3,2,1,0:T(8,128)(2,1)} %observed_h.1, f32[36,128,128]{2,1,0:T(8,128)} %basis_h.1, s32[4,8]{1,0:T(4,128)} %pick.1, s32[4]{0:T(128)} %count.1, f32[36,128]{1,0:T(8,128)} %bitcast.2, s32[4]{0:T(128)} %incoming.1, f32[72,128]{1,0:T(8,128)} %constant.18.clone.mask, ...), custom_call_target="tpu_custom_call" | custom-call | flops 30000001024 | bytes 10000000 | tf_op jit(solution)/shard_map/pallas_call | solution.py:619
  75.0 1.7 %shard_map.159 = (f32[4,128,128]{2,1,0:T(8,128)}, f32[36,128]{1,0:T(8,128)}) custom-call(f32[4,128,128]{2,1,0:T(8,128)} %get-tuple-element.6.objects, f32[36,128]{1,0:T(8,128)} %get-tuple-element.7.coef), custom_call_target="tpu_custom_call" | custom-call | flops 500000 | bytes 700000 | tf_op jit(solution)/shard_map/pallas_call | solution.py:679

commit v10 on v9

--- a/solution.py
+++ b/solution.py
@@ -405,7 +405,7 @@
         t1_h, t2_h, a2_h, a2t_h, w1_h, w1t_h,
         out, coef_out,
         observed, relay, window, basis, picks, picked, onehot, used, coef, own, t1, t2, a2, a2t, w1, w1t,
-        spec, basis6, six, phi, dphi, field, amp, trans, cot, grads, objects, near, send, arrive,
+        spec, basis6, six, phi, dphi, field, amp, trans, cot, halves, grads, objects, near, send, arrive,
         ob_send, ob_recv, pk_send, pk_recv, gr_send, gr_recv, ag_send, ag_recv, nb_send, nb_recv, basis_sem, load_sem,
     ):
         t, s = lax.axis_index("tile"), lax.axis_index("spare")
@@ -414,9 +414,10 @@
         groups = [
             [(t, v) for v in spare_of] + [(t + 1 - 2 * tc, (s + d) % 4) for d in range(4)],
             [(((tx + d) % 4) * 8 + tz * 2 + tc, s) for d in (1, 2, 3)],
-            [(tx * 8 + ((tz + d) % 4) * 2 + tc, s) for d in (1, 2, 3)],
+            [(tx * 8 + ((tz + d) % 4) * 2 + tc, s) for d in (1, 2, 3)]
+            + [(tx * 8 + ((tz + d) % 4) * 2 + 1 - tc, s) for d in range(4)],
         ]
-        places = [tc * 4 + s, tx, tz]
+        places = [tc * 4 + s, tx, tc * 4 + tz]
         beside = [((t + 1) % 32, s), ((t + 31) % 32, s)]
 
         barrier = pltpu.get_barrier_semaphore()
@@ -477,7 +478,8 @@
 
         def grad_copy(it, stage, d):
             here = grads.at[it, stage, places[stage]]
-            return remote(here, here, gr_send.at[it, stage, d], gr_recv.at[it, stage, d], groups[stage][d])
+            src = halves.at[it, tc if d < 3 else 1 - tc] if stage == 0 else here
+            return remote(src, here, gr_send.at[it, stage, d], gr_recv.at[it, stage, d], groups[stage][d])
 
         lane = lax.broadcasted_iota(jnp.int32, (8, 128), 1)
         row = lax.broadcasted_iota(jnp.int32, (8, 128), 0)
@@ -559,16 +561,25 @@
             for part in split3(slot_grad):
                 one = mm(part.astype(BF16), twice)
                 total = one if total is None else total + one
+            halves[it, 0] = total[:24]
+            halves[it, 1] = jnp.concatenate([total[24:], jnp.zeros((8, 128), F32)], axis=0)
+            half = halves[it, tc]
             for stage in range(3):
-                grads[it, stage, places[stage]] = total
+                grads[it, stage, places[stage]] = half
                 count = len(groups[stage])
                 for d in range(count):
                     grad_copy(it, stage, d).start()
                 for d in range(count):
                     grad_copy(it, stage, d).wait()
-                total = grads[it, stage, 0]
-                for d in range(count):
-                    total = total + grads[it, stage, d + 1]
+                if stage < 2:
+                    half = grads[it, stage, 0]
+                    for d in range(count):
+                        half = half + grads[it, stage, d + 1]
+            both = [
+                grads[it, 2, 4 * c] + grads[it, 2, 4 * c + 1] + grads[it, 2, 4 * c + 2] + grads[it, 2, 4 * c + 3]
+                for c in range(2)
+            ]
+            total = jnp.concatenate([both[0], both[1][:16]], axis=0)
             mean = jnp.sum(total * total) * (1.0 / (128.0 * 36.0))
             coef[...] = coef[...] - STEP * total / jnp.sqrt(jnp.full(total.shape, mean + EPS, F32))
 
@@ -650,7 +661,8 @@
             pltpu.VMEM((2 * QUADS, 256, 256), F32),
             pltpu.VMEM((QUADS, 256, 256), F32),
             pltpu.VMEM((3, 128, 128), F32),
-            pltpu.VMEM((ITERS, 3, 8, MROWS, 128), F32),
+            pltpu.VMEM((ITERS, 2, 24, 128), F32),
+            pltpu.VMEM((ITERS, 3, 8, 24, 128), F32),
             pltpu.VMEM((4, 128, 128), F32),
             pltpu.VMEM((2, 8, 128), jnp.int32),
             pltpu.VMEM((2, 128, 128), F32),

time: 76.9 us -> 77.5 us (level)
  no operation moved by 1% of the time
where the time goes in v10:
time: 77.5 us; the launch traced here: 77.3 us
  Pallas kernels  76.6 us (99%)
    pallas_call x1, Pallas kernels, per_device(): pl.pallas_call(make_kernel(), out_shape=(jax.ShapeDtypeStruct((4, NPIX, N...  74.9 us
    pallas_call x1, Pallas kernels, per_device(): pl.pallas_call(hand_on, out_shape=(jax.ShapeDtypeStruct((4, NPIX, NPIX),...  1.68 us

profile of v10, /device:TPU:1, one launch (start us, length us, event | category | flops | bytes accessed | tf_op | source)
XLA Modules:
  0.0 77.3 jit_solution(15781548963644223511)
XLA Ops:
  0.6 74.9 %shard_map.158 = (f32[4,128,128]{2,1,0:T(8,128)}, f32[36,128]{1,0:T(8,128)}) custom-call(bf16[4,8,128,128]{3,2,1,0:T(8,128)(2,1)} %observed_h.1, f32[36,128,128]{2,1,0:T(8,128)} %basis_h.1, s32[4,8]{1,0:T(4,128)} %pick.1, s32[4]{0:T(128)} %count.1, f32[36,128]{1,0:T(8,128)} %bitcast.2, s32[4]{0:T(128)} %incoming.1, f32[72,128]{1,0:T(8,128)} %constant.18.clone.mask, ...), custom_call_target="tpu_custom_call" | custom-call | flops 30000001024 | bytes 10000000 | tf_op jit(solution)/shard_map/pallas_call | solution.py:630
  75.6 1.7 %shard_map.159 = (f32[4,128,128]{2,1,0:T(8,128)}, f32[36,128]{1,0:T(8,128)}) custom-call(f32[4,128,128]{2,1,0:T(8,128)} %get-tuple-element.6.objects, f32[36,128]{1,0:T(8,128)} %get-tuple-element.7.coef), custom_call_target="tpu_custom_call" | custom-call | flops 500000 | bytes 700000 | tf_op jit(solution)/shard_map/pallas_call | solution.py:691

commit v11 on v9

--- a/solution.py
+++ b/solution.py
@@ -413,10 +413,13 @@
         spare_of = [(s + d) % 4 for d in (1, 2, 3)]
         groups = [
             [(t, v) for v in spare_of] + [(t + 1 - 2 * tc, (s + d) % 4) for d in range(4)],
-            [(((tx + d) % 4) * 8 + tz * 2 + tc, s) for d in (1, 2, 3)],
-            [(tx * 8 + ((tz + d) % 4) * 2 + tc, s) for d in (1, 2, 3)],
+            [
+                (((tx + dx) % 4) * 8 + ((tz + dz) % 4) * 2 + tc, s)
+                for dx, dz in [(1, 0), (0, 1), (3, 0), (0, 3), (1, 1), (3, 3), (1, 3), (3, 1), (2, 0), (0, 2)]
+                + [(2, 1), (1, 2), (2, 3), (3, 2), (2, 2)]
+            ],
         ]
-        places = [tc * 4 + s, tx, tz]
+        places = [tc * 4 + s, 4 * tx + tz]
         beside = [((t + 1) % 32, s), ((t + 31) % 32, s)]
 
         barrier = pltpu.get_barrier_semaphore()
@@ -559,7 +562,7 @@
             for part in split3(slot_grad):
                 one = mm(part.astype(BF16), twice)
                 total = one if total is None else total + one
-            for stage in range(3):
+            for stage in range(2):
                 grads[it, stage, places[stage]] = total
                 count = len(groups[stage])
                 for d in range(count):
@@ -650,7 +653,7 @@
             pltpu.VMEM((2 * QUADS, 256, 256), F32),
             pltpu.VMEM((QUADS, 256, 256), F32),
             pltpu.VMEM((3, 128, 128), F32),
-            pltpu.VMEM((ITERS, 3, 8, MROWS, 128), F32),
+            pltpu.VMEM((ITERS, 2, 16, MROWS, 128), F32),
             pltpu.VMEM((4, 128, 128), F32),
             pltpu.VMEM((2, 8, 128), jnp.int32),
             pltpu.VMEM((2, 128, 128), F32),
@@ -659,8 +662,8 @@
             dma((3, 2)),
             dma((3,)),
             dma((3,)),
-            dma((ITERS, 3, 7)),
-            dma((ITERS, 3, 7)),
+            dma((ITERS, 2, 15)),
+            dma((ITERS, 2, 15)),
             dma((3,)),
             dma((3,)),
             dma((2, 2)),

time: 76.9 us -> 79.6 us (1.035)
  Pallas kernels: 76.1 us -> 78.8 us
    pallas_call x1, Pallas kernels: 74.4 us -> 77.1 us  [per_device(): pl.pallas_call(make_kernel(), out_shape=(jax.ShapeDtypeStruct((4, NPIX, N...]
where the time goes in v11:
time: 79.6 us; the launch traced here: 79.4 us
  Pallas kernels  78.8 us (99%)
    pallas_call x1, Pallas kernels, per_device(): pl.pallas_call(make_kernel(), out_shape=(jax.ShapeDtypeStruct((4, NPIX, N...  77.1 us
    pallas_call x1, Pallas kernels, per_device(): pl.pallas_call(hand_on, out_shape=(jax.ShapeDtypeStruct((4, NPIX, NPIX),...  1.68 us

profile of v11, /device:TPU:1, one launch (start us, length us, event | category | flops | bytes accessed | tf_op | source)
XLA Modules:
  0.0 79.4 jit_solution(1832721436847711860)
XLA Ops:
  0.6 77.1 %shard_map.158 = (f32[4,128,128]{2,1,0:T(8,128)}, f32[36,128]{1,0:T(8,128)}) custom-call(bf16[4,8,128,128]{3,2,1,0:T(8,128)(2,1)} %observed_h.1, f32[36,128,128]{2,1,0:T(8,128)} %basis_h.1, s32[4,8]{1,0:T(4,128)} %pick.1, s32[4]{0:T(128)} %count.1, f32[36,128]{1,0:T(8,128)} %bitcast.2, s32[4]{0:T(128)} %incoming.1, f32[72,128]{1,0:T(8,128)} %constant.18.clone.mask, ...), custom_call_target="tpu_custom_call" | custom-call | flops 30000001024 | bytes 10000000 | tf_op jit(solution)/shard_map/pallas_call | solution.py:622
  77.7 1.7 %shard_map.159 = (f32[4,128,128]{2,1,0:T(8,128)}, f32[36,128]{1,0:T(8,128)}) custom-call(f32[4,128,128]{2,1,0:T(8,128)} %get-tuple-element.6.objects, f32[36,128]{1,0:T(8,128)} %get-tuple-element.7.coef), custom_call_target="tpu_custom_call" | custom-call | flops 500000 | bytes 700000 | tf_op jit(solution)/shard_map/pallas_call | solution.py:682
